TPU v7x, 1024 devices: a whole 4x4x32 slice. The times are simulated.
1024 devices in a mesh: row: 32 (over z), col: 32 (over x, y, core).
Axes of the slice: x: 4, y: 4, z: 32, core: 2. Of those that a mesh axis runs over, the one named last changes fastest.
Arguments:
- features: bfloat16 [65536, 512], P(('col', 'row')), may hold values from -6 to 6
- block_index: int32 [32, 32, 16], P('row', 'col'), may hold values from 0 to 255, as said below
- block_count: int32 [32, 32], P('row', 'col'), may hold values from 4 to 16, as said below
- block_values: bfloat16 [32, 32, 16, 128, 128], P('row', 'col'), may hold values from -0.3125 to 0.3125
- weight: bfloat16 [512, 512], replicated, may hold values from -0.25 to 0.25
- bias: float32 [512], replicated, may hold values from -3 to 3
Outputs:
- activated: bfloat16 [65536, 512], P(('row', 'col'))
Inputs may be any that keep to these rules, and one draw needn't show every extreme that they name: `block_index`: within one tile all 16 entries are distinct. `block_count`: some tile holds exactly 16 live slots.
All inputs are finite; a program needn't handle non-finite values.
Results may differ from a plain program's by a relative error of at most 0.02.
Values may be sent and summed in bfloat16 or wider, within the bound.
No kernel may reach another device: no remote copies, remote signals or barrier semaphores. Data moves between devices by JAX's collectives and lax.ppermute only.
A program may use at most 32 MiB of HBM per device.

v0:
```python
import jax
import jax.numpy as jnp
from jax import lax
from jax.sharding import PartitionSpec as P


def block_sums(tile_values, picked, select):
    products = jnp.einsum("bij,bjf->bif", tile_values, picked, preferred_element_type=jnp.float32)
    upper = products.astype(jnp.bfloat16)
    lower = (products - upper.astype(jnp.float32)).astype(jnp.bfloat16)
    select_half = select.astype(jnp.bfloat16)
    summed = jnp.einsum("rb,bif->rif", select_half, upper, preferred_element_type=jnp.float32)
    summed = summed + jnp.einsum(
        "rb,bif->rif", select_half, lower, preferred_element_type=jnp.float32
    )
    return summed.reshape(summed.shape[0] * summed.shape[1], summed.shape[2]).astype(jnp.bfloat16)


def local(features, block_index, block_count, block_values, weight, bias):
    column_panel = lax.all_gather(features, "row", axis=0, tiled=True)
    slot_index = block_index[0, 0]
    live_count = block_count[0, 0]
    tile_values = block_values[0, 0]
    slot_total = tile_values.shape[0]
    block_side = tile_values.shape[1]
    feat_width = column_panel.shape[1]
    send_blocks = column_panel.shape[0] // block_side
    recv_blocks = features.shape[0] * lax.axis_size("col") // block_side
    block_row = slot_index // send_blocks
    block_col = slot_index % send_blocks
    picked = column_panel.reshape(send_blocks, block_side, feat_width)[block_col]
    slot_ids = jnp.arange(slot_total, dtype=jnp.int32)
    row_ids = jnp.arange(recv_blocks, dtype=jnp.int32)
    select = ((block_row[None, :] == row_ids[:, None]) & (slot_ids[None, :] < live_count)).astype(
        jnp.float32
    )
    partial_sums = block_sums(tile_values, picked, select)
    summed = lax.psum_scatter(partial_sums, "col", scatter_dimension=0, tiled=True).astype(
        jnp.float32
    )
    aggregate = summed.astype(jnp.bfloat16)
    mixed = jnp.dot(aggregate, weight, preferred_element_type=jnp.float32) + bias
    return jax.nn.relu(mixed).astype(jnp.bfloat16)


def solution(mesh):
    return jax.shard_map(
        local,
        mesh=mesh,
        in_specs=(
            P(("col", "row"), None),
            P("row", "col", None),
            P("row", "col"),
            P("row", "col", None, None, None),
            P(),
            P(),
        ),
        out_specs=P(("row", "col"), None),
        check_vma=False,
    )
```

profile of v0, /device:TPU:1, one launch (start us, length us, event | category | flops | bytes accessed | tf_op | source)
XLA Modules:
  0.0 306.6 jit_solution(15348386924948985736)
XLA Ops:
  6.5 0.0 copy-start
  6.5 0.0 all-gather.2.cloned.1.call-start
  6.5 0.7 all-gather.2.cloned.1.call-update
  7.3 0.0 reduce-scatter.2.cloned.1.call-start
  8.0 0.7 fusion.15
  8.6 0.7 and_select_fusion.1
  9.3 127.4 %all-gather.2.cloned.1.call-done = bf16[2048,512]{1,0:T(8,128)(2,1)} async-done(((bf16[64,512]{1,0:T(8,128)(2,1)}), bf16[2048,512]{1,0:T(8,128)(2,1)}) %all-gather.2.cloned.1.call-update) | async-done | bytes 2097168 | tf_op jit(solution)/shard_map/all_gather | solution.py:20
  136.7 2.3 gather_fusion
  139.0 0.0 copy-done
  139.0 2.9 fusion
  141.9 3.4 %copy.11 = bf16[16,128,512]{2,0,1:T(8,128)(2,1)S(1)} copy(bf16[16,128,512]{1,2,0:T(8,128)(2,1)} %get-tuple-element.5) | data formatting | bytes 4194304 | tf_op jit(solution)/shard_map/convert_element_type | solution.py:10
  145.4 4.6 %copy.10 = bf16[16,128,512]{2,0,1:T(8,128)(2,1)} copy(bf16[16,128,512]{1,2,0:T(8,128)(2,1)} %get-tuple-element.6) | data formatting | bytes 4194304 | tf_op jit(solution)/shard_map/convert_element_type | solution.py:9
  149.9 2.3 fusion.8
  152.2 0.7 add_convert_fusion
  152.9 2.5 copy.12
  155.4 0.0 copy-start.1
  155.4 0.0 copy-start.2
  155.4 0.0 reduce-scatter.2.cloned.1.call-update
  155.4 142.6 %reduce-scatter.2.cloned.1.call-done = bf16[64,512]{1,0:T(8,128)(2,1)} async-done(((bf16[2048,512]{1,0:T(8,128)(2,1)}), bf16[64,512]{1,0:T(8,128)(2,1)}) %reduce-scatter.2.cloned.1.call-update) | async-done | bytes 65552 | tf_op jit(solution)/shard_map/reduce_scatter | solution.py:38
  298.1 0.0 copy-done.1
  298.1 0.0 copy-done.2
  298.1 1.7 fusion.2
  (2 shorter events, 0.0 us)
Async XLA Ops:
  6.5 132.5 %copy-start = (bf16[1,1,16,128,128]{4,3,2,1,0:T(8,128)(2,1)S(1)}, bf16[1,1,16,128,128]{4,3,2,1,0:T(8,128)(2,1)}, u32[]{:S(2)}) copy-start(bf16[1,1,16,128,128]{4,3,2,1,0:T(8,128)(2,1)} %param.9) | copy-start | bytes 1572868
  6.5 130.2 %all-gather.2.cloned.1.call-start = ((), (), s32[]{:S(2)}) async-start(), calls=%async_computation.1 | async-start | bytes 2162688 | tf_op jit(solution)/shard_map/all_gather | solution.py:20
  7.3 290.8 %reduce-scatter.2.cloned.1.call-start = ((), (), s32[]{:S(2)}) async-start(), calls=%async_computation.2 | async-start | bytes 2162688 | tf_op jit(solution)/shard_map/reduce_scatter | solution.py:38
  155.4 142.6 %copy-start.1 = (bf16[512,512]{1,0:T(8,128)(2,1)S(1)}, bf16[512,512]{1,0:T(8,128)(2,1)}, u32[]{:S(2)}) copy-start(bf16[512,512]{1,0:T(8,128)(2,1)} %param.10) | copy-start | bytes 1572868
  155.4 142.6 %copy-start.2 = (f32[512]{0:T(512)S(1)}, f32[512]{0:T(512)}, u32[]{:S(2)}) copy-start(f32[512]{0:T(512)} %param.11) | copy-start | bytes 6148
Sparse Core Ops, SparseCore 0:
  10.0 126.6 all-gather.1
  155.6 142.4 reduce-scatter.1
where the time goes:
time: 308 us; the launch traced here: 307 us
  waiting for transfers between devices  271 us (88%)
  between operations  14.1 us (5%)
  local copies, waits for them, and re-layouts  12.8 us (4%)
  matrix products  7.56 us (2%)
    reduce_scatter x1, waiting for transfers between devices, local(): lax.psum_scatter(partial_sums, 'col', scatter_dimension=0, tiled=True)  143 us
    all_gather x1, waiting for transfers between devices, local(): column_panel = lax.all_gather(features, 'row', axis=0, tiled=True)  127 us
  transfers between devices with their start and end apart: 2, of which 2 were waited for; matrix products, arithmetic and copies ran while one was open for 0% of the time, Pallas kernels for 0%

commit v1 on v0

v1 whole, which is shorter than its diff:
```python
import functools

import jax
import jax.numpy as jnp
from jax import lax
from jax.experimental import pallas as pl
from jax.experimental.pallas import tpu as pltpu
from jax.sharding import Mesh, PartitionSpec as P

STRIDE = 4
Z = ("zo", "zi")
XY = ("x", "y")


def tile_kernel(
    index_ref, count_ref, values_ref, own_ref, below_ref, above_ref, low_ref, high_ref,
    mine_ref, theirs_ref, panel, total,
):
    place, core = lax.axis_index("zi"), lax.axis_index("core")
    slots, side = values_ref.shape[2], values_ref.shape[3]
    dests, shard, _ = mine_ref.shape
    send_blocks = panel.shape[0] // side

    def put(ref, step, first):
        start = lax.rem(place + step, STRIDE)
        for k in range(ref.shape[0] // shard):
            row = pl.multiple_of((start + STRIDE * (first + k)) * shard, shard)
            panel[pl.ds(row, shard), :] = ref[k * shard : (k + 1) * shard, :]

    put(own_ref, 0, 0)
    put(above_ref, 1, 0)
    put(low_ref, 2, 0)
    put(high_ref, 2, low_ref.shape[0] // shard)
    put(below_ref, STRIDE - 1, 0)
    total[...] = jnp.zeros_like(total)
    for s in range(slots):
        place_in_tile = index_ref[0, 0, s]
        block_row = place_in_tile // send_blocks
        block_col = place_in_tile % send_blocks

        @pl.when(s < count_ref[0, 0])
        def _():
            rows = pl.ds(pl.multiple_of(block_row * side, side), side)
            nodes = pl.ds(pl.multiple_of(block_col * side, side), side)
            total[rows, :] += jnp.dot(
                values_ref[0, 0, s], panel[nodes, :], preferred_element_type=jnp.float32
            )

    for d in range(dests):
        for ref, who in ((mine_ref, core), (theirs_ref, 1 - core)):
            row = pl.multiple_of((2 * d + who) * shard, shard)
            ref[d] = total[pl.ds(row, shard), :].astype(ref.dtype)


def final_kernel(parts_ref, weight_ref, bias_ref, out_ref):
    aggregate = jnp.sum(parts_ref[...].astype(jnp.float32), axis=0).astype(jnp.bfloat16)
    mixed = jnp.dot(aggregate, weight_ref[...], preferred_element_type=jnp.float32)
    out_ref[...] = jnp.maximum(mixed + bias_ref[...], 0.0).astype(out_ref.dtype)


def local(features, block_index, block_count, block_values, weight, bias):
    shard, feat = features.shape
    rows = lax.axis_size("zo")
    z_size = rows * STRIDE
    xy_size = lax.axis_size("x") * lax.axis_size("y")

    def shift(array, by):
        return lax.ppermute(array, Z, [(z, (z + by) % z_size) for z in range(z_size)])

    own = lax.all_gather(features, "zo", axis=0, tiled=True)
    half = own.shape[0] // 2
    low = shift(own[:half], 2)
    high = shift(own[half:], -2)
    below = shift(own, 1)
    above = shift(own, -1)

    smem = pl.BlockSpec(memory_space=pltpu.SMEM)
    vmem = pl.BlockSpec(memory_space=pltpu.VMEM)
    half_sums = jax.ShapeDtypeStruct((xy_size, shard, feat), jnp.bfloat16)
    slots, side = block_values.shape[2], block_values.shape[3]
    mine, theirs = pl.pallas_call(
        tile_kernel,
        out_shape=(half_sums, half_sums),
        in_specs=[smem, smem] + [vmem] * 6,
        out_specs=(vmem, vmem),
        scratch_shapes=[
            pltpu.VMEM((z_size * shard, feat), jnp.bfloat16),
            pltpu.VMEM((2 * xy_size * shard, feat), jnp.float32),
        ],
        compiler_params=pltpu.CompilerParams(vmem_limit_bytes=40 * 1024 * 1024),
        cost_estimate=pl.CostEstimate(
            flops=2 * slots * side * side * feat,
            bytes_accessed=slots * side * side * 2 + z_size * shard * feat * 4,
            transcendentals=0,
        ),
    )(block_index, block_count, block_values, own, below, above, low, high)

    sibling = lax.ppermute(theirs, "core", [(0, 1), (1, 0)])
    pair = (mine.astype(jnp.float32) + sibling.astype(jnp.float32)).astype(jnp.bfloat16)
    parts = lax.all_to_all(pair, XY, 0, 0, tiled=True)
    return pl.pallas_call(
        final_kernel,
        out_shape=jax.ShapeDtypeStruct((shard, weight.shape[1]), jnp.bfloat16),
        in_specs=[vmem] * 3,
        out_specs=vmem,
        compiler_params=pltpu.CompilerParams(vmem_limit_bytes=40 * 1024 * 1024),
    )(parts, weight, bias.reshape(1, -1))


def solution(mesh):
    z_size, col = mesh.devices.shape
    side = int(round((col // 2) ** 0.5))
    grid = Mesh(
        mesh.devices.reshape(z_size // STRIDE, STRIDE, side, col // 2 // side, 2),
        Z + XY + ("core",),
    )
    column = XY + ("core",)
    return jax.shard_map(
        local,
        mesh=grid,
        in_specs=(
            P(column + Z, None),
            P(Z, column, None),
            P(Z, column),
            P(Z, column, None, None, None),
            P(),
            P(),
        ),
        out_specs=P(Z + column, None),
        check_vma=False,
    )
```

time: 308 us -> 118 us (0.38)
  the two profiles are of different devices: /device:TPU:1 before, /device:TPU:32 now
where the time goes in v1:
time: 118 us; the launch traced here: 117 us
  blocking collectives  83.5 us (71%)
  waiting for transfers between devices  15.1 us (13%)
  starting transfers between devices  14.5 us (12%)
  Pallas kernels  3.09 us (3%)
    all_gather x1, blocking collectives, local(): own = lax.all_gather(features, 'zo', axis=0, tiled=True)  59.1 us
    all_to_all x1, blocking collectives, local(): parts = lax.all_to_all(pair, XY, 0, 0, tiled=True)  24.3 us
    ppermute x4, starting transfers between devices, shift(): lax.ppermute(array, Z, [(z, (z + by) % z_size) for z in range(z_size)])  12.6 us
    ppermute x4, waiting for transfers between devices, shift(): lax.ppermute(array, Z, [(z, (z + by) % z_size) for z in range(z_size)])  12.4 us
    ppermute x1, waiting for transfers between devices, local(): sibling = lax.ppermute(theirs, 'core', [(0, 1), (1, 0)])  2.63 us
  transfers between devices with their start and end apart: 5, of which 3 were waited for; matrix products, arithmetic and copies ran while one was open for 0% of the time, Pallas kernels for 0%

profile of v1, /device:TPU:32, one launch (start us, length us, event | category | flops | bytes accessed | tf_op | source)
XLA Modules:
  0.0 117.2 jit_solution(12305775130719341273)
XLA Ops:
  0.0 0.0 copy-start
  0.0 0.0 copy-start.3
  0.0 59.1 %all_gather.3.own_ref = bf16[512,512]{1,0:T(8,128)(2,1)S(1)} all-gather(bf16[64,512]{1,0:T(8,128)(2,1)} %param.6), channel_id=1, replica_groups=mesh['zo'=8,'zi'=4,'x'=4,'y'=4,'core'=2] {'zo'}, dimensions={0}, use_global_device_ids=true | all-gather | bytes 589824 | tf_op jit(solution)/shard_map/all_gather | solution.py:70
  59.1 1.9 %collective-permute-start.1 = (bf16[512,512]{1,0:T(8,128)(2,1)S(1)}, bf16[512,512]{1,0:T(8,128)(2,1)S(1)}, u32[]{:S(2)}, u32[]{:S(2)}) collective-permute-start(bf16[512,512]{1,0:T(8,128)(2,1)S(1)} %all_gather.3.own_ref), channel_id=1, source_target_pairs={{0,992},{32,0},{64,32},{96,64},{128,96},{160,128},{192,160},{224,1... | collective-permute-start | bytes 1572872 | tf_op jit(solution)/shard_map/ppermute | solution.py:68
  61.1 3.9 %collective-permute-start = (bf16[512,512]{1,0:T(8,128)(2,1)S(1)}, bf16[512,512]{1,0:T(8,128)(2,1)S(1)}, u32[]{:S(2)}, u32[]{:S(2)}) collective-permute-start(bf16[512,512]{1,0:T(8,128)(2,1)S(1)} %all_gather.3.own_ref), channel_id=1, source_target_pairs={{0,32},{32,64},{64,96},{96,128},{128,160},{160,192},{192,224},{224... | collective-permute-start | bytes 1572872 | tf_op jit(solution)/shard_map/ppermute | solution.py:68
  65.0 3.4 %collective-permute-start.3 = (bf16[256,512]{1,0:T(8,128)(2,1)S(1)}, bf16[256,512]{1,0:T(8,128)(2,1)S(1)}, u32[]{:S(2)}, u32[]{:S(2)}) collective-permute-start(bf16[256,512]{1,0:T(8,128)(2,1)S(1)} %get-tuple-element.9), channel_id=1, source_target_pairs={{0,960},{32,992},{64,0},{96,32},{128,64},{160,96},{192,128},{224,1... | collective-permute-start | bytes 786440 | tf_op jit(solution)/shard_map/ppermute | solution.py:68
  68.5 3.3 %collective-permute-start.2 = (bf16[256,512]{1,0:T(8,128)(2,1)S(1)}, bf16[256,512]{1,0:T(8,128)(2,1)S(1)}, u32[]{:S(2)}, u32[]{:S(2)}) collective-permute-start(bf16[256,512]{1,0:T(8,128)(2,1)S(1)} %get-tuple-element.10), channel_id=1, source_target_pairs={{0,64},{32,96},{64,128},{96,160},{128,192},{160,224},{192,256},{22... | collective-permute-start | bytes 786440 | tf_op jit(solution)/shard_map/ppermute | solution.py:68
  72.4 4.5 %collective-permute-done.3.high_ref = bf16[256,512]{1,0:T(8,128)(2,1)S(1)} collective-permute-done((bf16[256,512]{1,0:T(8,128)(2,1)S(1)}, bf16[256,512]{1,0:T(8,128)(2,1)S(1)}, u32[]{:S(2)}, u32[]{:S(2)}) %collective-permute-start.3) | collective-permute-done | bytes 262176 | tf_op jit(solution)/shard_map/ppermute | solution.py:68
  77.0 7.9 %collective-permute-done.2.low_ref = bf16[256,512]{1,0:T(8,128)(2,1)S(1)} collective-permute-done((bf16[256,512]{1,0:T(8,128)(2,1)S(1)}, bf16[256,512]{1,0:T(8,128)(2,1)S(1)}, u32[]{:S(2)}, u32[]{:S(2)}) %collective-permute-start.2) | collective-permute-done | bytes 262176 | tf_op jit(solution)/shard_map/ppermute | solution.py:68
  84.9 0.0 collective-permute-done.1.above_ref
  84.9 0.0 collective-permute-done.below_ref
  84.9 0.0 copy-done
  84.9 0.0 copy-done.3
  84.9 2.2 %shard_map.64 = (bf16[16,64,512]{2,1,0:T(8,128)(2,1)S(1)}, bf16[16,64,512]{2,1,0:T(8,128)(2,1)S(1)}) custom-call(s32[1,1,16]{2,1,0:T(1,128)S(1)} %copy-done.3, s32[1,1]{1,0:T(1,128)S(6)} %copy.7.count_ref, bf16[1,1,16,128,128]{4,3,2,1,0:T(8,128)(2,1)S(1)} %copy-done, bf16[512,512]{1,0:T(8,128)(2,1)S(1)} %all_gather.3.own_ref, ...), custom_call_target="tpu_custom_call" | custom-call | flops 268435456 | bytes 4718592 | tf_op jit(solution)/shard_map/pallas_call | solution.py:81
  87.1 1.9 %collective-permute-start.4 = (bf16[16,64,512]{2,1,0:T(8,128)(2,1)S(1)}, bf16[16,64,512]{2,1,0:T(8,128)(2,1)S(1)}, u32[]{:S(2)}, u32[]{:S(2)}) collective-permute-start(bf16[16,64,512]{2,1,0:T(8,128)(2,1)S(1)} %get-tuple-element.8), channel_id=1, source_target_pairs={{0,1},{1,0},{2,3},{3,2},{4,5},{5,4},{6,7},{7,6},{8,9},{9,8},{10,11... | collective-permute-start | bytes 3145736 | tf_op jit(solution)/shard_map/ppermute | solution.py:98
  89.0 2.6 %collective-permute-done.4 = bf16[16,64,512]{2,1,0:T(8,128)(2,1)S(1)} collective-permute-done((bf16[16,64,512]{2,1,0:T(8,128)(2,1)S(1)}, bf16[16,64,512]{2,1,0:T(8,128)(2,1)S(1)}, u32[]{:S(2)}, u32[]{:S(2)}) %collective-permute-start.4) | collective-permute-done | bytes 1048608 | tf_op jit(solution)/shard_map/ppermute | solution.py:98
  91.6 0.3 add_convert_fusion
  92.0 0.0 copy-start.1
  92.0 0.0 copy-start.2
  92.0 24.3 %all_to_all.5.parts_ref = bf16[16,64,512]{2,1,0:T(8,128)(2,1)S(1)} all-to-all(bf16[16,64,512]{2,1,0:T(8,128)(2,1)S(1)} %add_convert_fusion), channel_id=1, replica_groups=mesh['zo'=8,'zi'=4,'x'=4,'y'=4,'core'=2] {'x','y'}, dimensions={0} | all-to-all | bytes 2097152 | tf_op jit(solution)/shard_map/all_to_all | solution.py:100
  116.3 0.0 copy-done.1
  116.3 0.0 copy-done.2
  116.3 0.9 shard_map.65
  (1 shorter events, 0.0 us)
Async XLA Ops:
  0.0 84.9 %copy-start = (bf16[1,1,16,128,128]{4,3,2,1,0:T(8,128)(2,1)S(1)}, bf16[1,1,16,128,128]{4,3,2,1,0:T(8,128)(2,1)}, u32[]{:S(2)}) copy-start(bf16[1,1,16,128,128]{4,3,2,1,0:T(8,128)(2,1)} %values_ref.1) | copy-start | bytes 1572868
  0.0 84.9 %copy-start.3 = (s32[1,1,16]{2,1,0:T(1,128)S(1)}, s32[1,1,16]{2,1,0:T(1,128)}, u32[]{:S(2)}) copy-start(s32[1,1,16]{2,1,0:T(1,128)} %index_ref.1) | copy-start | bytes 196
  59.1 25.7 %collective-permute-start.1 = (bf16[512,512]{1,0:T(8,128)(2,1)S(1)}, bf16[512,512]{1,0:T(8,128)(2,1)S(1)}, u32[]{:S(2)}, u32[]{:S(2)}) collective-permute-start(bf16[512,512]{1,0:T(8,128)(2,1)S(1)} %all_gather.3.own_ref), channel_id=1, source_target_pairs={{0,992},{32,0},{64,32},{96,64},{128,96},{160,128},{192,160},{224,1... | collective-permute-start | bytes 1572872 | tf_op jit(solution)/shard_map/ppermute | solution.py:68
  61.1 23.8 %collective-permute-start = (bf16[512,512]{1,0:T(8,128)(2,1)S(1)}, bf16[512,512]{1,0:T(8,128)(2,1)S(1)}, u32[]{:S(2)}, u32[]{:S(2)}) collective-permute-start(bf16[512,512]{1,0:T(8,128)(2,1)S(1)} %all_gather.3.own_ref), channel_id=1, source_target_pairs={{0,32},{32,64},{64,96},{96,128},{128,160},{160,192},{192,224},{224... | collective-permute-start | bytes 1572872 | tf_op jit(solution)/shard_map/ppermute | solution.py:68
  65.0 11.9 %collective-permute-start.3 = (bf16[256,512]{1,0:T(8,128)(2,1)S(1)}, bf16[256,512]{1,0:T(8,128)(2,1)S(1)}, u32[]{:S(2)}, u32[]{:S(2)}) collective-permute-start(bf16[256,512]{1,0:T(8,128)(2,1)S(1)} %get-tuple-element.9), channel_id=1, source_target_pairs={{0,960},{32,992},{64,0},{96,32},{128,64},{160,96},{192,128},{224,1... | collective-permute-start | bytes 786440 | tf_op jit(solution)/shard_map/ppermute | solution.py:68
  68.5 16.4 %collective-permute-start.2 = (bf16[256,512]{1,0:T(8,128)(2,1)S(1)}, bf16[256,512]{1,0:T(8,128)(2,1)S(1)}, u32[]{:S(2)}, u32[]{:S(2)}) collective-permute-start(bf16[256,512]{1,0:T(8,128)(2,1)S(1)} %get-tuple-element.10), channel_id=1, source_target_pairs={{0,64},{32,96},{64,128},{96,160},{128,192},{160,224},{192,256},{22... | collective-permute-start | bytes 786440 | tf_op jit(solution)/shard_map/ppermute | solution.py:68
  87.1 4.6 %collective-permute-start.4 = (bf16[16,64,512]{2,1,0:T(8,128)(2,1)S(1)}, bf16[16,64,512]{2,1,0:T(8,128)(2,1)S(1)}, u32[]{:S(2)}, u32[]{:S(2)}) collective-permute-start(bf16[16,64,512]{2,1,0:T(8,128)(2,1)S(1)} %get-tuple-element.8), channel_id=1, source_target_pairs={{0,1},{1,0},{2,3},{3,2},{4,5},{5,4},{6,7},{7,6},{8,9},{9,8},{10,11... | collective-permute-start | bytes 3145736 | tf_op jit(solution)/shard_map/ppermute | solution.py:98
  92.0 24.3 %copy-start.1 = (bf16[512,512]{1,0:T(8,128)(2,1)S(1)}, bf16[512,512]{1,0:T(8,128)(2,1)}, u32[]{:S(2)}) copy-start(bf16[512,512]{1,0:T(8,128)(2,1)} %weight_ref.1) | copy-start | bytes 1572868
  92.0 24.3 %copy-start.2 = (f32[512]{0:T(512)S(1)}, f32[512]{0:T(512)}, u32[]{:S(2)}) copy-start(f32[512]{0:T(512)} %param.11) | copy-start | bytes 6148

commit v2 on v1

--- a/solution.py
+++ b/solution.py
@@ -13,7 +13,7 @@
 
 
 def tile_kernel(
-    index_ref, count_ref, values_ref, own_ref, below_ref, above_ref, low_ref, high_ref,
+    index_ref, count_ref, values_ref, own_ref, below_ref, above_ref, far_ref,
     mine_ref, theirs_ref, panel, total,
 ):
     place, core = lax.axis_index("zi"), lax.axis_index("core")
@@ -21,17 +21,11 @@
     dests, shard, _ = mine_ref.shape
     send_blocks = panel.shape[0] // side
 
-    def put(ref, step, first):
+    for step, ref in enumerate((own_ref, above_ref, far_ref, below_ref)):
         start = lax.rem(place + step, STRIDE)
         for k in range(ref.shape[0] // shard):
-            row = pl.multiple_of((start + STRIDE * (first + k)) * shard, shard)
+            row = pl.multiple_of((start + STRIDE * k) * shard, shard)
             panel[pl.ds(row, shard), :] = ref[k * shard : (k + 1) * shard, :]
-
-    put(own_ref, 0, 0)
-    put(above_ref, 1, 0)
-    put(low_ref, 2, 0)
-    put(high_ref, 2, low_ref.shape[0] // shard)
-    put(below_ref, STRIDE - 1, 0)
     total[...] = jnp.zeros_like(total)
     for s in range(slots):
         place_in_tile = index_ref[0, 0, s]
@@ -68,9 +62,12 @@
         return lax.ppermute(array, Z, [(z, (z + by) % z_size) for z in range(z_size)])
 
     own = lax.all_gather(features, "zo", axis=0, tiled=True)
-    half = own.shape[0] // 2
-    low = shift(own[:half], 2)
-    high = shift(own[half:], -2)
+    pairs = [(z, core) for z in range(z_size) for core in range(2)]
+    far = lax.ppermute(
+        own,
+        Z + ("core",),
+        [(2 * z + c, 2 * ((z - 2 + 4 * c) % z_size) + c) for z, c in pairs],
+    )
     below = shift(own, 1)
     above = shift(own, -1)
 
@@ -81,7 +78,7 @@
     mine, theirs = pl.pallas_call(
         tile_kernel,
         out_shape=(half_sums, half_sums),
-        in_specs=[smem, smem] + [vmem] * 6,
+        in_specs=[smem, smem] + [vmem] * 5,
         out_specs=(vmem, vmem),
         scratch_shapes=[
             pltpu.VMEM((z_size * shard, feat), jnp.bfloat16),
@@ -93,7 +90,7 @@
             bytes_accessed=slots * side * side * 2 + z_size * shard * feat * 4,
             transcendentals=0,
         ),
-    )(block_index, block_count, block_values, own, below, above, low, high)
+    )(block_index, block_count, block_values, own, below, above, far)
 
     sibling = lax.ppermute(theirs, "core", [(0, 1), (1, 0)])
     pair = (mine.astype(jnp.float32) + sibling.astype(jnp.float32)).astype(jnp.bfloat16)

time: 118 us -> 117 us (level)
  the two profiles are of different devices: /device:TPU:32 before, /device:TPU:1 now
where the time goes in v2:
time: 117 us; the launch traced here: 116 us
  blocking collectives  75 us (64%)
  waiting for transfers between devices  19.3 us (16%)
  starting transfers between devices  15.3 us (13%)
  Pallas kernels  3.58 us (3%)
  local copies, waits for them, and re-layouts  1.71 us (1%)
    all_gather x1, blocking collectives, local(): own = lax.all_gather(features, 'zo', axis=0, tiled=True)  53 us
    all_to_all x1, blocking collectives, local(): parts = lax.all_to_all(pair, XY, 0, 0, tiled=True)  22 us
    ppermute x2, waiting for transfers between devices, shift(): lax.ppermute(array, Z, [(z, (z + by) % z_size) for z in range(z_size)])  13 us
    ppermute x1, starting transfers between devices, local(): sibling = lax.ppermute(theirs, 'core', [(0, 1), (1, 0)])  6.16 us
    ppermute x2, starting transfers between devices, shift(): lax.ppermute(array, Z, [(z, (z + by) % z_size) for z in range(z_size)])  5.54 us
    ppermute x1, waiting for transfers between devices, local(): lax.ppermute(own, Z + ('core',), [(2 * z + c, 2 * ((z - 2 + 4 * c) % z_si...  4.04 us
    ppermute x1, starting transfers between devices, local(): lax.ppermute(own, Z + ('core',), [(2 * z + c, 2 * ((z - 2 + 4 * c) % z_si...  3.65 us
    pallas_call x1, Pallas kernels, local(): pl.pallas_call(tile_kernel, out_shape=(half_sums, half_sums), in_specs=[s...  2.66 us
  transfers between devices with their start and end apart: 4, of which 4 were waited for; matrix products, arithmetic and copies ran while one was open for 0% of the time, Pallas kernels for 0%

profile of v2, /device:TPU:1, one launch (start us, length us, event | category | flops | bytes accessed | tf_op | source)
XLA Modules:
  0.0 116.0 jit_solution(582080466123983140)
XLA Ops:
  0.0 53.0 %all_gather.3.own_ref = bf16[512,512]{1,0:T(8,128)(2,1)S(1)} all-gather(bf16[64,512]{1,0:T(8,128)(2,1)} %param.6), channel_id=1, replica_groups=mesh['zo'=8,'zi'=4,'x'=4,'y'=4,'core'=2] {'zo'}, dimensions={0}, use_global_device_ids=true | all-gather | bytes 589824 | tf_op jit(solution)/shard_map/all_gather | solution.py:64
  53.0 3.7 %collective-permute-start.2 = (bf16[512,512]{1,0:T(8,128)(2,1)S(1)}, bf16[512,512]{1,0:T(8,128)(2,1)S(1)}, u32[]{:S(2)}, u32[]{:S(2)}) collective-permute-start(bf16[512,512]{1,0:T(8,128)(2,1)S(1)} %all_gather.3.own_ref), channel_id=1, source_target_pairs={{0,960},{1,65},{32,992},{33,97},{64,0},{65,129},{96,32},{97,161},{... | collective-permute-start | bytes 1572872 | tf_op jit(solution)/shard_map/ppermute | solution.py:66
  56.6 2.3 %collective-permute-start.1 = (bf16[512,512]{1,0:T(8,128)(2,1)S(1)}, bf16[512,512]{1,0:T(8,128)(2,1)S(1)}, u32[]{:S(2)}, u32[]{:S(2)}) collective-permute-start(bf16[512,512]{1,0:T(8,128)(2,1)S(1)} %all_gather.3.own_ref), channel_id=1, source_target_pairs={{0,992},{32,0},{64,32},{96,64},{128,96},{160,128},{192,160},{224,1... | collective-permute-start | bytes 1572872 | tf_op jit(solution)/shard_map/ppermute | solution.py:62
  58.9 3.3 %collective-permute-start = (bf16[512,512]{1,0:T(8,128)(2,1)S(1)}, bf16[512,512]{1,0:T(8,128)(2,1)S(1)}, u32[]{:S(2)}, u32[]{:S(2)}) collective-permute-start(bf16[512,512]{1,0:T(8,128)(2,1)S(1)} %all_gather.3.own_ref), channel_id=1, source_target_pairs={{0,32},{32,64},{64,96},{96,128},{128,160},{160,192},{192,224},{224... | collective-permute-start | bytes 1572872 | tf_op jit(solution)/shard_map/ppermute | solution.py:62
  62.8 4.0 %collective-permute-done.2.far_ref = bf16[512,512]{1,0:T(8,128)(2,1)S(1)} collective-permute-done((bf16[512,512]{1,0:T(8,128)(2,1)S(1)}, bf16[512,512]{1,0:T(8,128)(2,1)S(1)}, u32[]{:S(2)}, u32[]{:S(2)}) %collective-permute-start.2) | collective-permute-done | bytes 524320 | tf_op jit(solution)/shard_map/ppermute | solution.py:66
  66.9 1.2 %collective-permute-done.1.above_ref = bf16[512,512]{1,0:T(8,128)(2,1)S(1)} collective-permute-done((bf16[512,512]{1,0:T(8,128)(2,1)S(1)}, bf16[512,512]{1,0:T(8,128)(2,1)S(1)}, u32[]{:S(2)}, u32[]{:S(2)}) %collective-permute-start.1) | collective-permute-done | bytes 524320 | tf_op jit(solution)/shard_map/ppermute | solution.py:62
  68.1 11.8 %collective-permute-done.below_ref = bf16[512,512]{1,0:T(8,128)(2,1)S(1)} collective-permute-done((bf16[512,512]{1,0:T(8,128)(2,1)S(1)}, bf16[512,512]{1,0:T(8,128)(2,1)S(1)}, u32[]{:S(2)}, u32[]{:S(2)}) %collective-permute-start) | collective-permute-done | bytes 524320 | tf_op jit(solution)/shard_map/ppermute | solution.py:62
  79.9 0.0 copy-start
  79.9 1.0 copy-done
  80.9 0.0 copy-start.3
  80.9 0.7 copy-done.3
  81.6 2.7 %shard_map.64 = (bf16[16,64,512]{2,1,0:T(8,128)(2,1)S(1)}, bf16[16,64,512]{2,1,0:T(8,128)(2,1)S(1)}) custom-call(s32[1,1,16]{2,1,0:T(1,128)S(1)} %copy-done.3, s32[1,1]{1,0:T(1,128)S(6)} %copy.7.count_ref, bf16[1,1,16,128,128]{4,3,2,1,0:T(8,128)(2,1)S(1)} %copy-done, bf16[512,512]{1,0:T(8,128)(2,1)S(1)} %all_gather.3.own_ref, ...), custom_call_target="tpu_custom_call" | custom-call | flops 268435456 | bytes 4718592 | tf_op jit(solution)/shard_map/pallas_call | solution.py:78
  84.2 6.2 %collective-permute-start.3 = (bf16[16,64,512]{2,1,0:T(8,128)(2,1)S(1)}, bf16[16,64,512]{2,1,0:T(8,128)(2,1)S(1)}, u32[]{:S(2)}, u32[]{:S(2)}) collective-permute-start(bf16[16,64,512]{2,1,0:T(8,128)(2,1)S(1)} %get-tuple-element.8), channel_id=1, source_target_pairs={{0,1},{1,0},{2,3},{3,2},{4,5},{5,4},{6,7},{7,6},{8,9},{9,8},{10,11... | collective-permute-start | bytes 3145736 | tf_op jit(solution)/shard_map/ppermute | solution.py:95
  90.4 2.3 %collective-permute-done.3 = bf16[16,64,512]{2,1,0:T(8,128)(2,1)S(1)} collective-permute-done((bf16[16,64,512]{2,1,0:T(8,128)(2,1)S(1)}, bf16[16,64,512]{2,1,0:T(8,128)(2,1)S(1)}, u32[]{:S(2)}, u32[]{:S(2)}) %collective-permute-start.3) | collective-permute-done | bytes 1048608 | tf_op jit(solution)/shard_map/ppermute | solution.py:95
  92.7 0.3 add_convert_fusion
  93.0 0.0 copy-start.1
  93.0 0.0 copy-start.2
  93.0 22.0 %all_to_all.5.parts_ref = bf16[16,64,512]{2,1,0:T(8,128)(2,1)S(1)} all-to-all(bf16[16,64,512]{2,1,0:T(8,128)(2,1)S(1)} %add_convert_fusion), channel_id=1, replica_groups=mesh['zo'=8,'zi'=4,'x'=4,'y'=4,'core'=2] {'x','y'}, dimensions={0} | all-to-all | bytes 2097152 | tf_op jit(solution)/shard_map/all_to_all | solution.py:97
  115.0 0.0 copy-done.1
  115.0 0.0 copy-done.2
  115.0 0.9 shard_map.65
Async XLA Ops:
  53.0 13.9 %collective-permute-start.2 = (bf16[512,512]{1,0:T(8,128)(2,1)S(1)}, bf16[512,512]{1,0:T(8,128)(2,1)S(1)}, u32[]{:S(2)}, u32[]{:S(2)}) collective-permute-start(bf16[512,512]{1,0:T(8,128)(2,1)S(1)} %all_gather.3.own_ref), channel_id=1, source_target_pairs={{0,960},{1,65},{32,992},{33,97},{64,0},{65,129},{96,32},{97,161},{... | collective-permute-start | bytes 1572872 | tf_op jit(solution)/shard_map/ppermute | solution.py:66
  56.6 11.4 %collective-permute-start.1 = (bf16[512,512]{1,0:T(8,128)(2,1)S(1)}, bf16[512,512]{1,0:T(8,128)(2,1)S(1)}, u32[]{:S(2)}, u32[]{:S(2)}) collective-permute-start(bf16[512,512]{1,0:T(8,128)(2,1)S(1)} %all_gather.3.own_ref), channel_id=1, source_target_pairs={{0,992},{32,0},{64,32},{96,64},{128,96},{160,128},{192,160},{224,1... | collective-permute-start | bytes 1572872 | tf_op jit(solution)/shard_map/ppermute | solution.py:62
  58.9 21.0 %collective-permute-start = (bf16[512,512]{1,0:T(8,128)(2,1)S(1)}, bf16[512,512]{1,0:T(8,128)(2,1)S(1)}, u32[]{:S(2)}, u32[]{:S(2)}) collective-permute-start(bf16[512,512]{1,0:T(8,128)(2,1)S(1)} %all_gather.3.own_ref), channel_id=1, source_target_pairs={{0,32},{32,64},{64,96},{96,128},{128,160},{160,192},{192,224},{224... | collective-permute-start | bytes 1572872 | tf_op jit(solution)/shard_map/ppermute | solution.py:62
  79.9 1.0 copy-start
  80.9 0.7 copy-start.3
  84.2 8.4 %collective-permute-start.3 = (bf16[16,64,512]{2,1,0:T(8,128)(2,1)S(1)}, bf16[16,64,512]{2,1,0:T(8,128)(2,1)S(1)}, u32[]{:S(2)}, u32[]{:S(2)}) collective-permute-start(bf16[16,64,512]{2,1,0:T(8,128)(2,1)S(1)} %get-tuple-element.8), channel_id=1, source_target_pairs={{0,1},{1,0},{2,3},{3,2},{4,5},{5,4},{6,7},{7,6},{8,9},{9,8},{10,11... | collective-permute-start | bytes 3145736 | tf_op jit(solution)/shard_map/ppermute | solution.py:95
  93.0 22.0 %copy-start.1 = (bf16[512,512]{1,0:T(8,128)(2,1)S(1)}, bf16[512,512]{1,0:T(8,128)(2,1)}, u32[]{:S(2)}) copy-start(bf16[512,512]{1,0:T(8,128)(2,1)} %weight_ref.1) | copy-start | bytes 1572868
  93.0 22.0 %copy-start.2 = (f32[512]{0:T(512)S(1)}, f32[512]{0:T(512)}, u32[]{:S(2)}) copy-start(f32[512]{0:T(512)} %param.11) | copy-start | bytes 6148

commit v3 on v2

v3 whole, which is shorter than its diff:
```python
import jax
import jax.numpy as jnp
from jax import lax
from jax.experimental import pallas as pl
from jax.experimental.pallas import tpu as pltpu
from jax.sharding import Mesh, PartitionSpec as P

STRIDE = 4
Z = ("zo", "zm", "zl")
XY = ("x", "y")


def tile_kernel(
    index_ref, count_ref, other_meta_ref, values_ref, other_values_ref,
    own_ref, above_ref, far_ref, below_ref, mine_ref, theirs_ref, panel, total,
):
    pair, core = lax.axis_index("zl"), lax.axis_index("core")
    place = 2 * lax.axis_index("zm") + pair
    slots, side = values_ref.shape[2], values_ref.shape[3]
    dests, shard, _ = mine_ref.shape
    dests = dests // 2
    send_blocks = panel.shape[0] // side

    for step, ref in enumerate((own_ref, above_ref, far_ref, below_ref)):
        start = lax.rem(place + step, STRIDE)
        for k in range(ref.shape[0] // shard):
            row = pl.multiple_of((start + STRIDE * k) * shard, shard)
            panel[pl.ds(row, shard), :] = ref[k * shard : (k + 1) * shard, :]

    def add_tile(values, place_of, count):
        total[...] = jnp.zeros_like(total)
        for s in range(slots):
            place_in_tile = place_of(s)
            block_row = place_in_tile // send_blocks
            block_col = place_in_tile % send_blocks

            @pl.when(s < count)
            def _():
                rows = pl.ds(pl.multiple_of(block_row * side, side), side)
                nodes = pl.ds(pl.multiple_of(block_col * side, side), side)
                total[rows, :] += jnp.dot(
                    values[0, 0, s], panel[nodes, :], preferred_element_type=jnp.float32
                )

    def store_tile(plane):
        for d in range(dests):
            for ref, who in ((mine_ref, core), (theirs_ref, 1 - core)):
                row = pl.multiple_of((2 * d + who) * shard, shard)
                ref[plane * dests + d] = total[pl.ds(row, shard), :].astype(ref.dtype)

    add_tile(values_ref, lambda s: index_ref[0, 0, s], count_ref[0, 0])
    store_tile(pair)
    add_tile(other_values_ref, lambda s: other_meta_ref[s], other_meta_ref[slots])
    store_tile(1 - pair)


def final_kernel(parts_ref, weight_ref, bias_ref, out_ref):
    half, width = parts_ref.shape[0] // 2, parts_ref.shape[2]
    mixed = bias_ref[...]
    for k in range(2):
        part = parts_ref[k * half : (k + 1) * half].astype(jnp.float32)
        aggregate = jnp.sum(part, axis=0).astype(jnp.bfloat16)
        mixed = mixed + jnp.dot(
            aggregate,
            weight_ref[k * width : (k + 1) * width, :],
            preferred_element_type=jnp.float32,
        )
    out_ref[...] = jnp.maximum(mixed, 0.0).astype(out_ref.dtype)


def local(features, block_index, block_count, block_values, weight, bias):
    shard, feat = features.shape
    width = feat // 2
    z_size = lax.axis_size("zo") * STRIDE
    xy_size = lax.axis_size("x") * lax.axis_size("y")
    pair = lax.axis_index("zl")

    def shift(array, by):
        return lax.ppermute(array, Z, [(z, (z + by) % z_size) for z in range(z_size)])

    def swap(array, axis):
        return lax.ppermute(array, axis, [(0, 1), (1, 0)])

    other_values = swap(block_values, "zl")
    own = lax.all_gather(features, "zo", axis=0, tiled=True)
    kept = lax.dynamic_slice_in_dim(own, pair * width, width, 1)
    given = lax.dynamic_slice_in_dim(own, (1 - pair) * width, width, 1)
    pairs = [(z, core) for z in range(z_size) for core in range(2)]
    far = lax.ppermute(
        kept,
        Z + ("core",),
        [(2 * z + c, 2 * ((z - 2 + 4 * c) % z_size) + c) for z, c in pairs],
    )
    below = shift(given, 1)
    above = shift(given, -1)
    meta = jnp.concatenate([block_index[0, 0], block_count[0]])
    meta, given = lax.optimization_barrier((meta, given))
    other_meta = swap(meta, "zl")

    smem = pl.BlockSpec(memory_space=pltpu.SMEM)
    vmem = pl.BlockSpec(memory_space=pltpu.VMEM)
    sums = jax.ShapeDtypeStruct((2 * xy_size, shard, width), jnp.bfloat16)
    slots, side = block_values.shape[2], block_values.shape[3]
    mine, theirs = pl.pallas_call(
        tile_kernel,
        out_shape=(sums, sums),
        in_specs=[smem] * 3 + [vmem] * 6,
        out_specs=(vmem, vmem),
        scratch_shapes=[
            pltpu.VMEM((z_size * shard, width), jnp.bfloat16),
            pltpu.VMEM((2 * xy_size * shard, width), jnp.float32),
        ],
        compiler_params=pltpu.CompilerParams(vmem_limit_bytes=24 * 1024 * 1024),
        cost_estimate=pl.CostEstimate(
            flops=2 * slots * side * side * feat,
            bytes_accessed=slots * side * side * 4 + z_size * shard * feat * 3,
            transcendentals=0,
        ),
    )(
        block_index, block_count, other_meta, block_values, other_values,
        kept, above, far, below,
    )

    sibling = swap(theirs, "core")
    both = (mine.astype(jnp.float32) + sibling.astype(jnp.float32)).astype(jnp.bfloat16)
    parts = lax.all_to_all(both, ("zl",) + XY, 0, 0, tiled=True)
    return pl.pallas_call(
        final_kernel,
        out_shape=jax.ShapeDtypeStruct((shard, weight.shape[1]), jnp.bfloat16),
        in_specs=[vmem] * 3,
        out_specs=vmem,
        compiler_params=pltpu.CompilerParams(vmem_limit_bytes=24 * 1024 * 1024),
    )(parts, weight, bias.reshape(1, -1))


def solution(mesh):
    z_size, col = mesh.devices.shape
    side = int(round((col // 2) ** 0.5))
    grid = Mesh(
        mesh.devices.reshape(z_size // STRIDE, STRIDE // 2, 2, side, col // 2 // side, 2),
        Z + XY + ("core",),
    )
    column = XY + ("core",)
    return jax.shard_map(
        local,
        mesh=grid,
        in_specs=(
            P(column + Z, None),
            P(Z, column, None),
            P(Z, column),
            P(Z, column, None, None, None),
            P(),
            P(),
        ),
        out_specs=P(Z + column, None),
        check_vma=False,
    )
```

time: 117 us -> 121 us (1.034)
  waiting for transfers between devices: 19.3 us -> 8.45 us
  starting transfers between devices: 15.3 us -> 22.6 us
  blocking collectives: 75 us -> 82 us
  Pallas kernels: 3.58 us -> 5.44 us
  local copies, waits for them, and re-layouts: 1.71 us -> 0.05 us
    ppermute x2, waiting for transfers between devices: 13 us -> 3.15 us  [shift(): lax.ppermute(array, Z, [(z, (z + by) % z_size) for z in range(z_size)])]
    ppermute x2 -> x4, starting transfers between devices: 9.81 us -> 16.1 us  [the longest x3 12.3 us: swap(): return lax.ppermute(array, axis, [(0, 1), (1, 0)])]
    all_gather x1, blocking collectives: 53 us -> 59 us  [local(): own = lax.all_gather(features, 'zo', axis=0, tiled=True)]
    pallas_call x1, Pallas kernels: 2.66 us -> 4.53 us  [local(): pl.pallas_call(tile_kernel, out_shape=(sums, sums), in_specs=[smem] * 3 +...]
    unnamed x8, local copies, waits for them, and re-layouts: 1.71 us -> 0.02 us
    ppermute x2 -> x4, waiting for transfers between devices: 6.3 us -> 5.3 us  [the longest x3 5.3 us: swap(): return lax.ppermute(array, axis, [(0, 1), (1, 0)])]
  transfers between devices with their start and end apart: 4 -> 6, of which waited for: 4 -> 3; matrix products, arithmetic and copies ran while one was open for 0% -> 0% of each run, Pallas kernels for 0% -> 0%
where the time goes in v3:
time: 121 us; the launch traced here: 120 us
  blocking collectives  82 us (68%)
  starting transfers between devices  22.6 us (19%)
  waiting for transfers between devices  8.45 us (7%)
  Pallas kernels  5.44 us (4%)
    all_gather x1, blocking collectives, local(): own = lax.all_gather(features, 'zo', axis=0, tiled=True)  59 us
    all_to_all x1, blocking collectives, local(): parts = lax.all_to_all(both, ('zl',) + XY, 0, 0, tiled=True)  23 us
    ppermute x3, starting transfers between devices, swap(): return lax.ppermute(array, axis, [(0, 1), (1, 0)])  12.3 us
    ppermute x2, starting transfers between devices, shift(): lax.ppermute(array, Z, [(z, (z + by) % z_size) for z in range(z_size)])  6.49 us
    ppermute x3, waiting for transfers between devices, swap(): return lax.ppermute(array, axis, [(0, 1), (1, 0)])  5.3 us
    pallas_call x1, Pallas kernels, local(): pl.pallas_call(tile_kernel, out_shape=(sums, sums), in_specs=[smem] * 3 +...  4.53 us
    ppermute x1, starting transfers between devices, local(): lax.ppermute(kept, Z + ('core',), [(2 * z + c, 2 * ((z - 2 + 4 * c) % z_s...  3.81 us
    ppermute x2, waiting for transfers between devices, shift(): lax.ppermute(array, Z, [(z, (z + by) % z_size) for z in range(z_size)])  3.15 us
  transfers between devices with their start and end apart: 6, of which 3 were waited for; matrix products, arithmetic and copies ran while one was open for 0% of the time, Pallas kernels for 0%

profile of v3, /device:TPU:1, one launch (start us, length us, event | category | flops | bytes accessed | tf_op | source)
XLA Modules:
  0.0 119.9 jit_solution(14567540338044588616)
XLA Ops:
  0.0 0.0 copy-start.1
  0.0 0.0 copy-start.3
  0.0 4.5 %collective-permute-start.1 = (bf16[1,1,16,128,128]{4,3,2,1,0:T(8,128)(2,1)}, bf16[1,1,16,128,128]{4,3,2,1,0:T(8,128)(2,1)S(1)}, u32[]{:S(2)}, u32[]{:S(2)}) collective-permute-start(bf16[1,1,16,128,128]{4,3,2,1,0:T(8,128)(2,1)} %values_ref.1), channel_id=1, source_target_pairs={{0,32},{32,0},{1,33},{33,1},{2,34},{34,2},{3,35},{35,3},{4,36},{36... | collective-permute-start | bytes 1572872 | tf_op jit(solution)/shard_map/ppermute | solution.py:82
  4.5 59.0 %all_gather.3 = bf16[512,512]{1,0:T(8,128)(2,1)S(1)} all-gather(bf16[64,512]{1,0:T(8,128)(2,1)} %param.6), channel_id=1, replica_groups=mesh['zo'=8,'zm'=2,'zl'=2,'x'=4,'y'=4,'core'=2] {'zo'}, dimensions={0}, use_global_device_ids=true | all-gather | bytes 589824 | tf_op jit(solution)/shard_map/all_gather | solution.py:85
  63.6 3.8 %collective-permute-start.3 = (bf16[512,256]{1,0:T(8,128)(2,1)S(1)}, bf16[512,256]{1,0:T(8,128)(2,1)S(1)}, u32[]{:S(2)}, u32[]{:S(2)}) collective-permute-start(bf16[512,256]{1,0:T(8,128)(2,1)S(1)} %get-tuple-element.11.own_ref), channel_id=1, source_target_pairs={{0,960},{1,65},{32,992},{33,97},{64,0},{65,129},{96,32},{97,161},{... | collective-permute-start | bytes 786440 | tf_op jit(solution)/shard_map/ppermute | solution.py:89
  67.4 1.9 %collective-permute-start.4 = (bf16[512,256]{1,0:T(8,128)(2,1)S(1)}, bf16[512,256]{1,0:T(8,128)(2,1)S(1)}, u32[]{:S(2)}, u32[]{:S(2)}) collective-permute-start(bf16[512,256]{1,0:T(8,128)(2,1)S(1)} %get-tuple-element.12), channel_id=1, source_target_pairs={{0,32},{32,64},{64,96},{96,128},{128,160},{160,192},{192,224},{224... | collective-permute-start | bytes 786440 | tf_op jit(solution)/shard_map/ppermute | solution.py:79
  69.3 4.6 %collective-permute-start.2 = (bf16[512,256]{1,0:T(8,128)(2,1)S(1)}, bf16[512,256]{1,0:T(8,128)(2,1)S(1)}, u32[]{:S(2)}, u32[]{:S(2)}) collective-permute-start(bf16[512,256]{1,0:T(8,128)(2,1)S(1)} %get-tuple-element.12), channel_id=1, source_target_pairs={{0,992},{32,0},{64,32},{96,64},{128,96},{160,128},{192,160},{224,1... | collective-permute-start | bytes 786440 | tf_op jit(solution)/shard_map/ppermute | solution.py:79
  74.5 0.0 copy-done.3
  74.5 0.1 pad_add_fusion
  74.6 1.9 %collective-permute-start = (s32[17]{0:T(128)S(1)}, s32[17]{0:T(128)S(1)}, u32[]{:S(2)}, u32[]{:S(2)}) collective-permute-start(s32[17]{0:T(128)S(1)} %pad_add_fusion), channel_id=1, source_target_pairs={{0,32},{32,0},{1,33},{33,1},{2,34},{34,2},{3,35},{35,3},{4,36},{36... | collective-permute-start | bytes 212 | tf_op jit(solution)/shard_map/ppermute | solution.py:82
  76.5 3.0 %collective-permute-done.other_meta_ref = s32[17]{0:T(128)S(1)} collective-permute-done((s32[17]{0:T(128)S(1)}, s32[17]{0:T(128)S(1)}, u32[]{:S(2)}, u32[]{:S(2)}) %collective-permute-start) | collective-permute-done | bytes 100 | tf_op jit(solution)/shard_map/ppermute | solution.py:82
  79.6 0.0 collective-permute-done.3.far_ref
  79.6 0.0 collective-permute-done.4.below_ref
  79.6 3.2 %collective-permute-done.2.above_ref = bf16[512,256]{1,0:T(8,128)(2,1)S(1)} collective-permute-done((bf16[512,256]{1,0:T(8,128)(2,1)S(1)}, bf16[512,256]{1,0:T(8,128)(2,1)S(1)}, u32[]{:S(2)}, u32[]{:S(2)}) %collective-permute-start.2) | collective-permute-done | bytes 262176 | tf_op jit(solution)/shard_map/ppermute | solution.py:79
  82.7 0.0 collective-permute-done.1.other_values_ref
  82.7 0.0 copy-done.1
  82.7 4.5 %shard_map.64 = (bf16[32,64,256]{2,1,0:T(8,128)(2,1)S(1)}, bf16[32,64,256]{2,1,0:T(8,128)(2,1)S(1)}) custom-call(s32[1,1,16]{2,1,0:T(1,128)S(1)} %copy-done.3, s32[1,1]{1,0:T(1,128)} %copy.7.count_ref, s32[17]{0:T(128)S(1)} %collective-permute-done.other_meta_ref, bf16[1,1,16,128,128]{4,3,2,1,0:T(8,128)(2,1)S(1)} %copy-done.1, ...), custom_call_target="tpu_custom_call" | custom-call | flops 268435456 | bytes 4194304 | tf_op jit(solution)/shard_map/pallas_call | solution.py:104
  87.3 5.9 %collective-permute-start.5 = (bf16[32,64,256]{2,1,0:T(8,128)(2,1)S(1)}, bf16[32,64,256]{2,1,0:T(8,128)(2,1)S(1)}, u32[]{:S(2)}, u32[]{:S(2)}) collective-permute-start(bf16[32,64,256]{2,1,0:T(8,128)(2,1)S(1)} %get-tuple-element.10), channel_id=1, source_target_pairs={{0,1},{1,0},{2,3},{3,2},{4,5},{5,4},{6,7},{7,6},{8,9},{9,8},{10,11... | collective-permute-start | bytes 3145736 | tf_op jit(solution)/shard_map/ppermute | solution.py:82
  93.2 2.3 %collective-permute-done.5 = bf16[32,64,256]{2,1,0:T(8,128)(2,1)S(1)} collective-permute-done((bf16[32,64,256]{2,1,0:T(8,128)(2,1)S(1)}, bf16[32,64,256]{2,1,0:T(8,128)(2,1)S(1)}, u32[]{:S(2)}, u32[]{:S(2)}) %collective-permute-start.5) | collective-permute-done | bytes 1048608 | tf_op jit(solution)/shard_map/ppermute | solution.py:82
  95.5 0.4 add_convert_fusion
  95.9 0.0 copy-start
  95.9 0.0 copy-start.2
  95.9 23.0 %all_to_all.5.parts_ref = bf16[32,64,256]{2,1,0:T(8,128)(2,1)S(1)} all-to-all(bf16[32,64,256]{2,1,0:T(8,128)(2,1)S(1)} %add_convert_fusion), channel_id=1, replica_groups=mesh['zo'=8,'zm'=2,'zl'=2,'x'=4,'y'=4,'core'=2] {'zl','x','y'}, dimensions={0} | all-to-all | bytes 2097152 | tf_op jit(solution)/shard_map/all_to_all | solution.py:126
  118.9 0.0 copy-done
  118.9 0.0 copy-done.2
  118.9 0.9 shard_map.65
  (1 shorter events, 0.0 us)
Async XLA Ops:
  0.0 82.7 %copy-start.1 = (bf16[1,1,16,128,128]{4,3,2,1,0:T(8,128)(2,1)S(1)}, bf16[1,1,16,128,128]{4,3,2,1,0:T(8,128)(2,1)}, u32[]{:S(2)}) copy-start(bf16[1,1,16,128,128]{4,3,2,1,0:T(8,128)(2,1)} %values_ref.1) | copy-start | bytes 1572868
  0.0 74.5 %copy-start.3 = (s32[1,1,16]{2,1,0:T(1,128)S(1)}, s32[1,1,16]{2,1,0:T(1,128)}, u32[]{:S(2)}) copy-start(s32[1,1,16]{2,1,0:T(1,128)} %index_ref.1) | copy-start | bytes 196
  0.0 82.7 %collective-permute-start.1 = (bf16[1,1,16,128,128]{4,3,2,1,0:T(8,128)(2,1)}, bf16[1,1,16,128,128]{4,3,2,1,0:T(8,128)(2,1)S(1)}, u32[]{:S(2)}, u32[]{:S(2)}) collective-permute-start(bf16[1,1,16,128,128]{4,3,2,1,0:T(8,128)(2,1)} %values_ref.1), channel_id=1, source_target_pairs={{0,32},{32,0},{1,33},{33,1},{2,34},{34,2},{3,35},{35,3},{4,36},{36... | collective-permute-start | bytes 1572872 | tf_op jit(solution)/shard_map/ppermute | solution.py:82
  63.6 16.0 %collective-permute-start.3 = (bf16[512,256]{1,0:T(8,128)(2,1)S(1)}, bf16[512,256]{1,0:T(8,128)(2,1)S(1)}, u32[]{:S(2)}, u32[]{:S(2)}) collective-permute-start(bf16[512,256]{1,0:T(8,128)(2,1)S(1)} %get-tuple-element.11.own_ref), channel_id=1, source_target_pairs={{0,960},{1,65},{32,992},{33,97},{64,0},{65,129},{96,32},{97,161},{... | collective-permute-start | bytes 786440 | tf_op jit(solution)/shard_map/ppermute | solution.py:89
  67.4 12.2 %collective-permute-start.4 = (bf16[512,256]{1,0:T(8,128)(2,1)S(1)}, bf16[512,256]{1,0:T(8,128)(2,1)S(1)}, u32[]{:S(2)}, u32[]{:S(2)}) collective-permute-start(bf16[512,256]{1,0:T(8,128)(2,1)S(1)} %get-tuple-element.12), channel_id=1, source_target_pairs={{0,32},{32,64},{64,96},{96,128},{128,160},{160,192},{192,224},{224... | collective-permute-start | bytes 786440 | tf_op jit(solution)/shard_map/ppermute | solution.py:79
  69.3 13.4 %collective-permute-start.2 = (bf16[512,256]{1,0:T(8,128)(2,1)S(1)}, bf16[512,256]{1,0:T(8,128)(2,1)S(1)}, u32[]{:S(2)}, u32[]{:S(2)}) collective-permute-start(bf16[512,256]{1,0:T(8,128)(2,1)S(1)} %get-tuple-element.12), channel_id=1, source_target_pairs={{0,992},{32,0},{64,32},{96,64},{128,96},{160,128},{192,160},{224,1... | collective-permute-start | bytes 786440 | tf_op jit(solution)/shard_map/ppermute | solution.py:79
  74.6 4.9 %collective-permute-start = (s32[17]{0:T(128)S(1)}, s32[17]{0:T(128)S(1)}, u32[]{:S(2)}, u32[]{:S(2)}) collective-permute-start(s32[17]{0:T(128)S(1)} %pad_add_fusion), channel_id=1, source_target_pairs={{0,32},{32,0},{1,33},{33,1},{2,34},{34,2},{3,35},{35,3},{4,36},{36... | collective-permute-start | bytes 212 | tf_op jit(solution)/shard_map/ppermute | solution.py:82
  87.3 8.2 %collective-permute-start.5 = (bf16[32,64,256]{2,1,0:T(8,128)(2,1)S(1)}, bf16[32,64,256]{2,1,0:T(8,128)(2,1)S(1)}, u32[]{:S(2)}, u32[]{:S(2)}) collective-permute-start(bf16[32,64,256]{2,1,0:T(8,128)(2,1)S(1)} %get-tuple-element.10), channel_id=1, source_target_pairs={{0,1},{1,0},{2,3},{3,2},{4,5},{5,4},{6,7},{7,6},{8,9},{9,8},{10,11... | collective-permute-start | bytes 3145736 | tf_op jit(solution)/shard_map/ppermute | solution.py:82
  95.9 23.0 %copy-start = (bf16[512,512]{1,0:T(8,128)(2,1)S(1)}, bf16[512,512]{1,0:T(8,128)(2,1)}, u32[]{:S(2)}) copy-start(bf16[512,512]{1,0:T(8,128)(2,1)} %weight_ref.1) | copy-start | bytes 1572868
  95.9 23.0 %copy-start.2 = (f32[512]{0:T(512)S(1)}, f32[512]{0:T(512)}, u32[]{:S(2)}) copy-start(f32[512]{0:T(512)} %param.11) | copy-start | bytes 6148

commit v4 on v2

v4 whole, which is shorter than its diff:
```python
import jax
import jax.numpy as jnp
from jax import lax
from jax.experimental import pallas as pl
from jax.experimental.pallas import tpu as pltpu
from jax.sharding import Mesh, PartitionSpec as P

STRIDE = 4
Z = ("zo", "zi")
XY = ("x", "y")
VMEM_LIMIT = 16 * 1024 * 1024


def each_live(index_ref, count_ref, slots, send_blocks, work):
    for s in range(slots):
        place_in_tile = index_ref[0, 0, s]
        pl.when(s < count_ref[0, 0])(
            lambda s=s, e=place_in_tile: work(s, e // send_blocks, e % send_blocks)
        )


def near_kernel(
    index_ref, count_ref, values_ref, own_ref, first_ref, second_ref, total_ref, panel
):
    place, core = lax.axis_index("zi"), lax.axis_index("core")
    slots, side = values_ref.shape[2], values_ref.shape[3]
    shard = panel.shape[0] // lax.axis_size("zo") // STRIDE
    classes = lax.axis_size("zo")
    send_blocks = panel.shape[0] // side

    steps = (0, STRIDE - 1 - 2 * core, 1 + 2 * core, 2)
    for step, ref in zip(steps, (own_ref, first_ref, second_ref, None)):
        start = lax.rem(place + step, STRIDE)
        for k in range(classes):
            rows = pl.ds(pl.multiple_of((start + STRIDE * k) * shard, shard), shard)
            if ref is None:
                panel[rows, :] = jnp.zeros((shard, panel.shape[1]), panel.dtype)
            else:
                panel[rows, :] = ref[k * shard : (k + 1) * shard, :]
    total_ref[...] = jnp.zeros_like(total_ref)

    def work(s, block_row, block_col):
        rows = pl.ds(pl.multiple_of(block_row * side, side), side)
        nodes = pl.ds(pl.multiple_of(block_col * side, side), side)
        total_ref[rows, :] += jnp.dot(
            values_ref[0, 0, s], panel[nodes, :], preferred_element_type=jnp.float32
        )

    each_live(index_ref, count_ref, slots, send_blocks, work)


def far_kernel(
    index_ref, count_ref, values_ref, far_ref, total_in_ref, total_ref, theirs_ref
):
    del total_in_ref
    place, core = lax.axis_index("zi"), lax.axis_index("core")
    slots, side = values_ref.shape[2], values_ref.shape[3]
    dests, shard, _ = theirs_ref.shape
    send_blocks = far_ref.shape[0] * STRIDE // side
    far_class = lax.rem(place + 2, STRIDE)
    per_block = side // shard

    for part in range(per_block):

        def work(s, block_row, block_col, part=part):
            node = block_col * per_block + part

            @pl.when(lax.rem(node, STRIDE) == far_class)
            def _():
                rows = pl.ds(pl.multiple_of(block_row * side, side), side)
                nodes = pl.ds(pl.multiple_of(node // STRIDE * shard, shard), shard)
                total_ref[rows, :] += jnp.dot(
                    values_ref[0, 0, s, :, part * shard : (part + 1) * shard],
                    far_ref[nodes, :],
                    preferred_element_type=jnp.float32,
                )

        @pl.when(lax.rem(far_class, per_block) == part)
        def _():
            each_live(index_ref, count_ref, slots, send_blocks, work)

    for d in range(dests):
        row = pl.multiple_of((2 * d + 1 - core) * shard, shard)
        theirs_ref[d] = total_ref[pl.ds(row, shard), :].astype(theirs_ref.dtype)


def pair_kernel(total_ref, sibling_ref, out_ref):
    core = lax.axis_index("core")
    dests, shard, _ = out_ref.shape
    for d in range(dests):
        row = pl.multiple_of((2 * d + core) * shard, shard)
        mine = total_ref[pl.ds(row, shard), :]
        out_ref[d] = (mine + sibling_ref[d].astype(jnp.float32)).astype(out_ref.dtype)


def final_kernel(parts_ref, weight_ref, bias_ref, out_ref):
    aggregate = jnp.sum(parts_ref[...].astype(jnp.float32), axis=0).astype(jnp.bfloat16)
    mixed = jnp.dot(aggregate, weight_ref[...], preferred_element_type=jnp.float32)
    out_ref[...] = jnp.maximum(mixed + bias_ref[...], 0.0).astype(out_ref.dtype)


def local(features, block_index, block_count, block_values, weight, bias):
    shard, feat = features.shape
    rows = lax.axis_size("zo")
    z_size = rows * STRIDE
    xy_size = lax.axis_size("x") * lax.axis_size("y")

    def turn(array, sign):
        return lax.ppermute(
            array,
            Z + ("core",),
            [
                (2 * z + c, 2 * ((z + sign * (1 - 2 * c)) % z_size) + c)
                for z in range(z_size)
                for c in range(2)
            ],
        )

    own = lax.all_gather(features, "zo", axis=0, tiled=True)
    first = turn(own, 1)
    second = turn(own, -1)
    far = turn(first, 1)

    smem = pl.BlockSpec(memory_space=pltpu.SMEM)
    vmem = pl.BlockSpec(memory_space=pltpu.VMEM)
    params = pltpu.CompilerParams(vmem_limit_bytes=VMEM_LIMIT)
    rows_all = 2 * xy_size * shard
    sums = jax.ShapeDtypeStruct((rows_all, feat), jnp.float32)
    half_sums = jax.ShapeDtypeStruct((xy_size, shard, feat), jnp.bfloat16)
    slots, side = block_values.shape[2], block_values.shape[3]

    def cost(share):
        return pl.CostEstimate(
            flops=int(2 * slots * side * side * feat * share),
            bytes_accessed=int(rows_all * feat * 8 * share),
            transcendentals=0,
        )

    total = pl.pallas_call(
        near_kernel,
        out_shape=sums,
        in_specs=[smem, smem] + [vmem] * 4,
        out_specs=vmem,
        scratch_shapes=[pltpu.VMEM((z_size * shard, feat), jnp.bfloat16)],
        compiler_params=params,
        cost_estimate=cost(0.75),
    )(block_index, block_count, block_values, own, first, second)
    total, theirs = pl.pallas_call(
        far_kernel,
        out_shape=(sums, half_sums),
        in_specs=[smem, smem] + [vmem] * 3,
        out_specs=(vmem, vmem),
        input_output_aliases={4: 0},
        compiler_params=params,
        cost_estimate=cost(0.25),
    )(block_index, block_count, block_values, far, total)
    sibling = lax.ppermute(theirs, "core", [(0, 1), (1, 0)])
    both = pl.pallas_call(
        pair_kernel,
        out_shape=half_sums,
        in_specs=[vmem] * 2,
        out_specs=vmem,
        compiler_params=params,
    )(total, sibling)
    parts = lax.all_to_all(both, XY, 0, 0, tiled=True)
    return pl.pallas_call(
        final_kernel,
        out_shape=jax.ShapeDtypeStruct((shard, weight.shape[1]), jnp.bfloat16),
        in_specs=[vmem] * 3,
        out_specs=vmem,
        compiler_params=params,
    )(parts, weight, bias.reshape(1, -1))


def solution(mesh):
    z_size, col = mesh.devices.shape
    side = int(round((col // 2) ** 0.5))
    grid = Mesh(
        mesh.devices.reshape(z_size // STRIDE, STRIDE, side, col // 2 // side, 2),
        Z + XY + ("core",),
    )
    column = XY + ("core",)
    return jax.shard_map(
        local,
        mesh=grid,
        in_specs=(
            P(column + Z, None),
            P(Z, column, None),
            P(Z, column),
            P(Z, column, None, None, None),
            P(),
            P(),
        ),
        out_specs=P(Z + column, None),
        check_vma=False,
    )
```

time: 117 us -> 116 us (level)
  waiting for transfers between devices: 19.3 us -> 14.1 us
  starting transfers between devices: 15.3 us -> 18.8 us
  Pallas kernels: 3.58 us -> 4.93 us
    ppermute x3, waiting for transfers between devices: 17 us -> 11.8 us  [turn(): lax.ppermute(array, Z + ('core',), [(2 * z + c, 2 * ((z + sign * (1 - 2 *...]
    ppermute x1, starting transfers between devices: 6.16 us -> 9.14 us  [local(): sibling = lax.ppermute(theirs, 'core', [(0, 1), (1, 0)])]
    pallas_call x1 -> x3, Pallas kernels: 2.66 us -> 4.02 us  [the longest x1 2.28 us: local(): pl.pallas_call(near_kernel, out_shape=sums, in_specs=[smem, smem] + [vmem...]
  transfers between devices with their start and end apart: 4 -> 4, of which waited for: 4 -> 4; matrix products, arithmetic and copies ran while one was open for 0% -> 0% of each run, Pallas kernels for 0% -> 2%
where the time goes in v4:
time: 116 us
  blocking collectives  75.8 us (65%)
  starting transfers between devices  18.8 us (16%)
  waiting for transfers between devices  14.1 us (12%)
  Pallas kernels  4.93 us (4%)
  local copies, waits for them, and re-layouts  1.7 us (1%)
    all_gather x1, blocking collectives, local(): own = lax.all_gather(features, 'zo', axis=0, tiled=True)  53 us
    all_to_all x1, blocking collectives, local(): parts = lax.all_to_all(both, XY, 0, 0, tiled=True)  22.8 us
    ppermute x3, waiting for transfers between devices, turn(): lax.ppermute(array, Z + ('core',), [(2 * z + c, 2 * ((z + sign * (1 - 2 *...  11.8 us
    ppermute x3, starting transfers between devices, turn(): lax.ppermute(array, Z + ('core',), [(2 * z + c, 2 * ((z + sign * (1 - 2 *...  9.7 us
    ppermute x1, starting transfers between devices, local(): sibling = lax.ppermute(theirs, 'core', [(0, 1), (1, 0)])  9.14 us
  transfers between devices with their start and end apart: 4, of which 4 were waited for; matrix products, arithmetic and copies ran while one was open for 0% of the time, Pallas kernels for 2%

profile of v4, /device:TPU:1, one launch (start us, length us, event | category | flops | bytes accessed | tf_op | source)
XLA Modules:
  0.0 116.0 jit_solution(18068347115316300728)
XLA Ops:
  0.0 53.0 %all_gather.3.own_ref = bf16[512,512]{1,0:T(8,128)(2,1)S(1)} all-gather(bf16[64,512]{1,0:T(8,128)(2,1)} %param.6), channel_id=1, replica_groups=mesh['zo'=8,'zi'=4,'x'=4,'y'=4,'core'=2] {'zo'}, dimensions={0}, use_global_device_ids=true | all-gather | bytes 589824 | tf_op jit(solution)/shard_map/all_gather | solution.py:119
  53.0 3.5 %collective-permute-start = (bf16[512,512]{1,0:T(8,128)(2,1)S(1)}, bf16[512,512]{1,0:T(8,128)(2,1)S(1)}, u32[]{:S(2)}, u32[]{:S(2)}) collective-permute-start(bf16[512,512]{1,0:T(8,128)(2,1)S(1)} %all_gather.3.own_ref), channel_id=1, source_target_pairs={{0,32},{1,993},{32,64},{33,1},{64,96},{65,33},{96,128},{97,65},{12... | collective-permute-start | bytes 1572872 | tf_op jit(solution)/shard_map/ppermute | solution.py:109
  56.4 1.9 %collective-permute-start.2 = (bf16[512,512]{1,0:T(8,128)(2,1)S(1)}, bf16[512,512]{1,0:T(8,128)(2,1)S(1)}, u32[]{:S(2)}, u32[]{:S(2)}) collective-permute-start(bf16[512,512]{1,0:T(8,128)(2,1)S(1)} %all_gather.3.own_ref), channel_id=1, source_target_pairs={{0,992},{1,33},{32,0},{33,65},{64,32},{65,97},{96,64},{97,129},{12... | collective-permute-start | bytes 1572872 | tf_op jit(solution)/shard_map/ppermute | solution.py:109
  58.4 5.0 %collective-permute-done.first_ref = bf16[512,512]{1,0:T(8,128)(2,1)S(1)} collective-permute-done((bf16[512,512]{1,0:T(8,128)(2,1)S(1)}, bf16[512,512]{1,0:T(8,128)(2,1)S(1)}, u32[]{:S(2)}, u32[]{:S(2)}) %collective-permute-start) | collective-permute-done | bytes 524320 | tf_op jit(solution)/shard_map/ppermute | solution.py:109
  63.4 4.3 %collective-permute-start.1 = (bf16[512,512]{1,0:T(8,128)(2,1)S(1)}, bf16[512,512]{1,0:T(8,128)(2,1)S(1)}, u32[]{:S(2)}, u32[]{:S(2)}) collective-permute-start(bf16[512,512]{1,0:T(8,128)(2,1)S(1)} %collective-permute-done.first_ref), channel_id=1, source_target_pairs={{0,32},{1,993},{32,64},{33,1},{64,96},{65,33},{96,128},{97,65},{12... | collective-permute-start | bytes 1572872 | tf_op jit(solution)/shard_map/ppermute | solution.py:109
  68.4 0.9 collective-permute-done.2.second_ref
  69.2 0.0 copy-start
  69.2 1.0 copy-done
  70.3 0.0 copy-start.3
  70.3 0.7 copy-done.3
  70.9 2.3 %shard_map.64.total_in_ref = f32[2048,512]{1,0:T(8,128)S(1)} custom-call(s32[1,1,16]{2,1,0:T(1,128)S(1)} %copy-done.3, s32[1,1]{1,0:T(1,128)S(6)} %copy.9.count_ref, bf16[1,1,16,128,128]{4,3,2,1,0:T(8,128)(2,1)S(1)} %copy-done, bf16[512,512]{1,0:T(8,128)(2,1)S(1)} %all_gather.3.own_ref, bf16[512,512]{1,0:T(8,128)(2,1)S(1)} %collective-permute-done.first_ref, ...), custom_call_target="tpu_custom_call" | custom-call | flops 201326592 | bytes 6291456 | tf_op jit(solution)/shard_map/pallas_call | solution.py:139
  73.2 5.9 %collective-permute-done.1.far_ref = bf16[512,512]{1,0:T(8,128)(2,1)S(1)} collective-permute-done((bf16[512,512]{1,0:T(8,128)(2,1)S(1)}, bf16[512,512]{1,0:T(8,128)(2,1)S(1)}, u32[]{:S(2)}, u32[]{:S(2)}) %collective-permute-start.1) | collective-permute-done | bytes 524320 | tf_op jit(solution)/shard_map/ppermute | solution.py:109
  79.1 1.5 %shard_map.65 = (f32[2048,512]{1,0:T(8,128)S(1)}, bf16[16,64,512]{2,1,0:T(8,128)(2,1)S(1)}) custom-call(s32[1,1,16]{2,1,0:T(1,128)S(1)} %copy-done.3, s32[1,1]{1,0:T(1,128)S(6)} %copy.9.count_ref, bf16[1,1,16,128,128]{4,3,2,1,0:T(8,128)(2,1)S(1)} %copy-done, bf16[512,512]{1,0:T(8,128)(2,1)S(1)} %collective-permute-done.1.far_ref, ...), custom_call_target="tpu_custom_call", output_to_operand_aliasing={{0}: (4, {})} | custom-call | flops 67108864 | bytes 2097152 | tf_op jit(solution)/shard_map/pallas_call | solution.py:148
  80.7 9.1 %collective-permute-start.3 = (bf16[16,64,512]{2,1,0:T(8,128)(2,1)S(1)}, bf16[16,64,512]{2,1,0:T(8,128)(2,1)S(1)}, u32[]{:S(2)}, u32[]{:S(2)}) collective-permute-start(bf16[16,64,512]{2,1,0:T(8,128)(2,1)S(1)} %get-tuple-element.8), channel_id=1, source_target_pairs={{0,1},{1,0},{2,3},{3,2},{4,5},{5,4},{6,7},{7,6},{8,9},{9,8},{10,11... | collective-permute-start | bytes 3145736 | tf_op jit(solution)/shard_map/ppermute | solution.py:157
  89.8 2.3 %collective-permute-done.3.sibling_ref = bf16[16,64,512]{2,1,0:T(8,128)(2,1)S(1)} collective-permute-done((bf16[16,64,512]{2,1,0:T(8,128)(2,1)S(1)}, bf16[16,64,512]{2,1,0:T(8,128)(2,1)S(1)}, u32[]{:S(2)}, u32[]{:S(2)}) %collective-permute-start.3) | collective-permute-done | bytes 1048608 | tf_op jit(solution)/shard_map/ppermute | solution.py:157
  92.1 0.0 copy-start.1
  92.1 0.0 copy-start.2
  92.1 0.2 shard_map.66
  92.3 22.8 %all_to_all.5.parts_ref = bf16[16,64,512]{2,1,0:T(8,128)(2,1)S(1)} all-to-all(bf16[16,64,512]{2,1,0:T(8,128)(2,1)S(1)} %shard_map.66), channel_id=1, replica_groups=mesh['zo'=8,'zi'=4,'x'=4,'y'=4,'core'=2] {'x','y'}, dimensions={0} | all-to-all | bytes 2097152 | tf_op jit(solution)/shard_map/all_to_all | solution.py:165
  115.1 0.0 copy-done.1
  115.1 0.0 copy-done.2
  115.1 0.9 shard_map.67
Async XLA Ops:
  53.0 10.4 %collective-permute-start = (bf16[512,512]{1,0:T(8,128)(2,1)S(1)}, bf16[512,512]{1,0:T(8,128)(2,1)S(1)}, u32[]{:S(2)}, u32[]{:S(2)}) collective-permute-start(bf16[512,512]{1,0:T(8,128)(2,1)S(1)} %all_gather.3.own_ref), channel_id=1, source_target_pairs={{0,32},{1,993},{32,64},{33,1},{64,96},{65,33},{96,128},{97,65},{12... | collective-permute-start | bytes 1572872 | tf_op jit(solution)/shard_map/ppermute | solution.py:109
  56.4 12.8 %collective-permute-start.2 = (bf16[512,512]{1,0:T(8,128)(2,1)S(1)}, bf16[512,512]{1,0:T(8,128)(2,1)S(1)}, u32[]{:S(2)}, u32[]{:S(2)}) collective-permute-start(bf16[512,512]{1,0:T(8,128)(2,1)S(1)} %all_gather.3.own_ref), channel_id=1, source_target_pairs={{0,992},{1,33},{32,0},{33,65},{64,32},{65,97},{96,64},{97,129},{12... | collective-permute-start | bytes 1572872 | tf_op jit(solution)/shard_map/ppermute | solution.py:109
  63.4 15.7 %collective-permute-start.1 = (bf16[512,512]{1,0:T(8,128)(2,1)S(1)}, bf16[512,512]{1,0:T(8,128)(2,1)S(1)}, u32[]{:S(2)}, u32[]{:S(2)}) collective-permute-start(bf16[512,512]{1,0:T(8,128)(2,1)S(1)} %collective-permute-done.first_ref), channel_id=1, source_target_pairs={{0,32},{1,993},{32,64},{33,1},{64,96},{65,33},{96,128},{97,65},{12... | collective-permute-start | bytes 1572872 | tf_op jit(solution)/shard_map/ppermute | solution.py:109
  69.2 1.0 copy-start
  70.3 0.7 copy-start.3
  80.7 11.4 %collective-permute-start.3 = (bf16[16,64,512]{2,1,0:T(8,128)(2,1)S(1)}, bf16[16,64,512]{2,1,0:T(8,128)(2,1)S(1)}, u32[]{:S(2)}, u32[]{:S(2)}) collective-permute-start(bf16[16,64,512]{2,1,0:T(8,128)(2,1)S(1)} %get-tuple-element.8), channel_id=1, source_target_pairs={{0,1},{1,0},{2,3},{3,2},{4,5},{5,4},{6,7},{7,6},{8,9},{9,8},{10,11... | collective-permute-start | bytes 3145736 | tf_op jit(solution)/shard_map/ppermute | solution.py:157
  92.1 23.0 %copy-start.1 = (bf16[512,512]{1,0:T(8,128)(2,1)S(1)}, bf16[512,512]{1,0:T(8,128)(2,1)}, u32[]{:S(2)}) copy-start(bf16[512,512]{1,0:T(8,128)(2,1)} %weight_ref.1) | copy-start | bytes 1572868
  92.1 23.0 %copy-start.2 = (f32[512]{0:T(512)S(1)}, f32[512]{0:T(512)}, u32[]{:S(2)}) copy-start(f32[512]{0:T(512)} %param.11) | copy-start | bytes 6148

commit v5 on v4

--- a/solution.py
+++ b/solution.py
@@ -15,12 +15,15 @@
     for s in range(slots):
         place_in_tile = index_ref[0, 0, s]
         pl.when(s < count_ref[0, 0])(
-            lambda s=s, e=place_in_tile: work(s, e // send_blocks, e % send_blocks)
+            lambda s=s, e=place_in_tile: work(
+                s, lax.div(e, send_blocks), lax.rem(e, send_blocks)
+            )
         )
 
 
 def near_kernel(
-    index_ref, count_ref, values_ref, own_ref, first_ref, second_ref, total_ref, panel
+    index_ref, count_ref, values_ref, own_ref, first_low_ref, first_high_ref, second_ref,
+    total_ref, panel,
 ):
     place, core = lax.axis_index("zi"), lax.axis_index("core")
     slots, side = values_ref.shape[2], values_ref.shape[3]
@@ -29,14 +32,16 @@
     send_blocks = panel.shape[0] // side
 
     steps = (0, STRIDE - 1 - 2 * core, 1 + 2 * core, 2)
-    for step, ref in zip(steps, (own_ref, first_ref, second_ref, None)):
+    sources = ((own_ref,), (first_low_ref, first_high_ref), (second_ref,), ())
+    for step, refs in zip(steps, sources):
         start = lax.rem(place + step, STRIDE)
+        shards = [r[k : k + shard, :] for r in refs for k in range(0, r.shape[0], shard)]
         for k in range(classes):
             rows = pl.ds(pl.multiple_of((start + STRIDE * k) * shard, shard), shard)
-            if ref is None:
+            if shards:
+                panel[rows, :] = shards[k]
+            else:
                 panel[rows, :] = jnp.zeros((shard, panel.shape[1]), panel.dtype)
-            else:
-                panel[rows, :] = ref[k * shard : (k + 1) * shard, :]
     total_ref[...] = jnp.zeros_like(total_ref)
 
     def work(s, block_row, block_col):
@@ -50,13 +55,17 @@
 
 
 def far_kernel(
-    index_ref, count_ref, values_ref, far_ref, total_in_ref, total_ref, theirs_ref
+    index_ref, count_ref, values_ref, far_low_ref, far_high_ref, total_in_ref,
+    total_ref, theirs_ref, far,
 ):
     del total_in_ref
     place, core = lax.axis_index("zi"), lax.axis_index("core")
     slots, side = values_ref.shape[2], values_ref.shape[3]
     dests, shard, _ = theirs_ref.shape
-    send_blocks = far_ref.shape[0] * STRIDE // side
+    send_blocks = far.shape[0] * STRIDE // side
+    half = far_low_ref.shape[0]
+    far[:half, :] = far_low_ref[...]
+    far[half:, :] = far_high_ref[...]
     far_class = lax.rem(place + 2, STRIDE)
     per_block = side // shard
 
@@ -68,10 +77,10 @@
             @pl.when(lax.rem(node, STRIDE) == far_class)
             def _():
                 rows = pl.ds(pl.multiple_of(block_row * side, side), side)
-                nodes = pl.ds(pl.multiple_of(node // STRIDE * shard, shard), shard)
+                nodes = pl.ds(pl.multiple_of(lax.div(node, STRIDE) * shard, shard), shard)
                 total_ref[rows, :] += jnp.dot(
                     values_ref[0, 0, s, :, part * shard : (part + 1) * shard],
-                    far_ref[nodes, :],
+                    far[nodes, :],
                     preferred_element_type=jnp.float32,
                 )
 
@@ -117,9 +126,10 @@
         )
 
     own = lax.all_gather(features, "zo", axis=0, tiled=True)
-    first = turn(own, 1)
+    cut = (lax.axis_size("zo") * 5 // 8) * shard
+    first = [turn(own[:cut], 1), turn(own[cut:], 1)]
     second = turn(own, -1)
-    far = turn(first, 1)
+    far = [turn(part, 1) for part in first]
 
     smem = pl.BlockSpec(memory_space=pltpu.SMEM)
     vmem = pl.BlockSpec(memory_space=pltpu.VMEM)
@@ -139,21 +149,22 @@
     total = pl.pallas_call(
         near_kernel,
         out_shape=sums,
-        in_specs=[smem, smem] + [vmem] * 4,
+        in_specs=[smem, smem] + [vmem] * 5,
         out_specs=vmem,
         scratch_shapes=[pltpu.VMEM((z_size * shard, feat), jnp.bfloat16)],
         compiler_params=params,
         cost_estimate=cost(0.75),
-    )(block_index, block_count, block_values, own, first, second)
+    )(block_index, block_count, block_values, own, *first, second)
     total, theirs = pl.pallas_call(
         far_kernel,
         out_shape=(sums, half_sums),
-        in_specs=[smem, smem] + [vmem] * 3,
+        in_specs=[smem, smem] + [vmem] * 4,
         out_specs=(vmem, vmem),
-        input_output_aliases={4: 0},
+        input_output_aliases={5: 0},
+        scratch_shapes=[pltpu.VMEM(own.shape, own.dtype)],
         compiler_params=params,
         cost_estimate=cost(0.25),
-    )(block_index, block_count, block_values, far, total)
+    )(block_index, block_count, block_values, *far, total)
     sibling = lax.ppermute(theirs, "core", [(0, 1), (1, 0)])
     both = pl.pallas_call(
         pair_kernel,

time: 116 us -> 114 us (0.983)
  waiting for transfers between devices: 14.1 us -> 4.15 us
  starting transfers between devices: 18.8 us -> 28 us
    ppermute x3 -> x5, waiting for transfers between devices: 11.8 us -> 1.88 us  [turn(): lax.ppermute(array, Z + ('core',), [(2 * z + c, 2 * ((z + sign * (1 - 2 *...]
    ppermute x3 -> x5, starting transfers between devices: 9.7 us -> 17.5 us  [turn(): lax.ppermute(array, Z + ('core',), [(2 * z + c, 2 * ((z + sign * (1 - 2 *...]
    ppermute x1, starting transfers between devices: 9.14 us -> 10.4 us  [local(): sibling = lax.ppermute(theirs, 'core', [(0, 1), (1, 0)])]
  transfers between devices with their start and end apart: 4 -> 6, of which waited for: 4 -> 2; matrix products, arithmetic and copies ran while one was open for 0% -> 0% of each run, Pallas kernels for 2% -> 2%
where the time goes in v5:
time: 114 us
  blocking collectives  74.7 us (66%)
  starting transfers between devices  28 us (25%)
  Pallas kernels  4.58 us (4%)
  waiting for transfers between devices  4.15 us (4%)
  local copies, waits for them, and re-layouts  1.74 us (2%)
    all_gather x1, blocking collectives, local(): own = lax.all_gather(features, 'zo', axis=0, tiled=True)  53 us
    all_to_all x1, blocking collectives, local(): parts = lax.all_to_all(both, XY, 0, 0, tiled=True)  21.8 us
    ppermute x5, starting transfers between devices, turn(): lax.ppermute(array, Z + ('core',), [(2 * z + c, 2 * ((z + sign * (1 - 2 *...  17.5 us
    ppermute x1, starting transfers between devices, local(): sibling = lax.ppermute(theirs, 'core', [(0, 1), (1, 0)])  10.4 us
  transfers between devices with their start and end apart: 6, of which 2 were waited for; matrix products, arithmetic and copies ran while one was open for 0% of the time, Pallas kernels for 2%

profile of v5, /device:TPU:1, one launch (start us, length us, event | category | flops | bytes accessed | tf_op | source)
XLA Modules:
  0.0 114.0 jit_solution(10441682433102915338)
XLA Ops:
  0.0 53.0 %all_gather.3.own_ref = bf16[512,512]{1,0:T(8,128)(2,1)S(1)} all-gather(bf16[64,512]{1,0:T(8,128)(2,1)} %param.6), channel_id=1, replica_groups=mesh['zo'=8,'zi'=4,'x'=4,'y'=4,'core'=2] {'zo'}, dimensions={0}, use_global_device_ids=true | all-gather | bytes 589824 | tf_op jit(solution)/shard_map/all_gather | solution.py:128
  53.0 3.5 %collective-permute-start = (bf16[320,512]{1,0:T(8,128)(2,1)S(1)}, bf16[320,512]{1,0:T(8,128)(2,1)S(1)}, u32[]{:S(2)}, u32[]{:S(2)}) collective-permute-start(bf16[320,512]{1,0:T(8,128)(2,1)S(1)} %slice.8), channel_id=1, source_target_pairs={{0,32},{1,993},{32,64},{33,1},{64,96},{65,33},{96,128},{97,65},{12... | collective-permute-start | bytes 983048 | tf_op jit(solution)/shard_map/ppermute | solution.py:118
  56.5 1.9 %collective-permute-start.4 = (bf16[512,512]{1,0:T(8,128)(2,1)S(1)}, bf16[512,512]{1,0:T(8,128)(2,1)S(1)}, u32[]{:S(2)}, u32[]{:S(2)}) collective-permute-start(bf16[512,512]{1,0:T(8,128)(2,1)S(1)} %all_gather.3.own_ref), channel_id=1, source_target_pairs={{0,992},{1,33},{32,0},{33,65},{64,32},{65,97},{96,64},{97,129},{12... | collective-permute-start | bytes 1572872 | tf_op jit(solution)/shard_map/ppermute | solution.py:118
  58.4 4.6 %collective-permute-start.2 = (bf16[192,512]{1,0:T(8,128)(2,1)S(1)}, bf16[192,512]{1,0:T(8,128)(2,1)S(1)}, u32[]{:S(2)}, u32[]{:S(2)}) collective-permute-start(bf16[192,512]{1,0:T(8,128)(2,1)S(1)} %slice.9), channel_id=1, source_target_pairs={{0,32},{1,993},{32,64},{33,1},{64,96},{65,33},{96,128},{97,65},{12... | collective-permute-start | bytes 589832 | tf_op jit(solution)/shard_map/ppermute | solution.py:118
  63.0 0.0 collective-permute-done.first_low_ref
  63.0 2.6 %collective-permute-start.1 = (bf16[320,512]{1,0:T(8,128)(2,1)S(1)}, bf16[320,512]{1,0:T(8,128)(2,1)S(1)}, u32[]{:S(2)}, u32[]{:S(2)}) collective-permute-start(bf16[320,512]{1,0:T(8,128)(2,1)S(1)} %collective-permute-done.first_low_ref), channel_id=1, source_target_pairs={{0,32},{1,993},{32,64},{33,1},{64,96},{65,33},{96,128},{97,65},{12... | collective-permute-start | bytes 983048 | tf_op jit(solution)/shard_map/ppermute | solution.py:118
  65.7 0.0 collective-permute-done.2.first_high_ref
  65.7 4.9 %collective-permute-start.3 = (bf16[192,512]{1,0:T(8,128)(2,1)S(1)}, bf16[192,512]{1,0:T(8,128)(2,1)S(1)}, u32[]{:S(2)}, u32[]{:S(2)}) collective-permute-start(bf16[192,512]{1,0:T(8,128)(2,1)S(1)} %collective-permute-done.2.first_high_ref), channel_id=1, source_target_pairs={{0,32},{1,993},{32,64},{33,1},{64,96},{65,33},{96,128},{97,65},{12... | collective-permute-start | bytes 589832 | tf_op jit(solution)/shard_map/ppermute | solution.py:118
  71.3 0.0 collective-permute-done.4.second_ref
  71.3 0.0 copy-start
  71.3 1.0 copy-done
  72.3 0.0 copy-start.3
  72.3 0.7 copy-done.3
  73.0 2.1 %shard_map.64.total_in_ref = f32[2048,512]{1,0:T(8,128)S(1)} custom-call(s32[1,1,16]{2,1,0:T(1,128)S(1)} %copy-done.3, s32[1,1]{1,0:T(1,128)S(6)} %copy.9.count_ref, bf16[1,1,16,128,128]{4,3,2,1,0:T(8,128)(2,1)S(1)} %copy-done, bf16[512,512]{1,0:T(8,128)(2,1)S(1)} %all_gather.3.own_ref, bf16[320,512]{1,0:T(8,128)(2,1)S(1)} %collective-permute-done.first_low_ref, ...), custom_call_target="tpu_custom_call" | custom-call | flops 201326592 | bytes 6291456 | tf_op jit(solution)/shard_map/pallas_call | solution.py:149
  75.1 1.9 %collective-permute-done.3.far_high_ref = bf16[192,512]{1,0:T(8,128)(2,1)S(1)} collective-permute-done((bf16[192,512]{1,0:T(8,128)(2,1)S(1)}, bf16[192,512]{1,0:T(8,128)(2,1)S(1)}, u32[]{:S(2)}, u32[]{:S(2)}) %collective-permute-start.3) | collective-permute-done | bytes 196640 | tf_op jit(solution)/shard_map/ppermute | solution.py:118
  77.0 0.0 collective-permute-done.1.far_low_ref
  77.0 1.3 %shard_map.65 = (f32[2048,512]{1,0:T(8,128)S(1)}, bf16[16,64,512]{2,1,0:T(8,128)(2,1)S(1)}) custom-call(s32[1,1,16]{2,1,0:T(1,128)S(1)} %copy-done.3, s32[1,1]{1,0:T(1,128)S(6)} %copy.9.count_ref, bf16[1,1,16,128,128]{4,3,2,1,0:T(8,128)(2,1)S(1)} %copy-done, ...), custom_call_target="tpu_custom_call", output_to_operand_aliasing={{0}: (5, {})} | custom-call | flops 67108864 | bytes 2097152 | tf_op jit(solution)/shard_map/pallas_call | solution.py:158
  78.3 10.4 %collective-permute-start.5 = (bf16[16,64,512]{2,1,0:T(8,128)(2,1)S(1)}, bf16[16,64,512]{2,1,0:T(8,128)(2,1)S(1)}, u32[]{:S(2)}, u32[]{:S(2)}) collective-permute-start(bf16[16,64,512]{2,1,0:T(8,128)(2,1)S(1)} %get-tuple-element.8), channel_id=1, source_target_pairs={{0,1},{1,0},{2,3},{3,2},{4,5},{5,4},{6,7},{7,6},{8,9},{9,8},{10,11... | collective-permute-start | bytes 3145736 | tf_op jit(solution)/shard_map/ppermute | solution.py:168
  88.8 2.3 %collective-permute-done.5.sibling_ref = bf16[16,64,512]{2,1,0:T(8,128)(2,1)S(1)} collective-permute-done((bf16[16,64,512]{2,1,0:T(8,128)(2,1)S(1)}, bf16[16,64,512]{2,1,0:T(8,128)(2,1)S(1)}, u32[]{:S(2)}, u32[]{:S(2)}) %collective-permute-start.5) | collective-permute-done | bytes 1048608 | tf_op jit(solution)/shard_map/ppermute | solution.py:168
  91.0 0.0 copy-start.1
  91.0 0.0 copy-start.2
  91.0 0.2 shard_map.66
  91.2 21.8 %all_to_all.5.parts_ref = bf16[16,64,512]{2,1,0:T(8,128)(2,1)S(1)} all-to-all(bf16[16,64,512]{2,1,0:T(8,128)(2,1)S(1)} %shard_map.66), channel_id=1, replica_groups=mesh['zo'=8,'zi'=4,'x'=4,'y'=4,'core'=2] {'x','y'}, dimensions={0} | all-to-all | bytes 2097152 | tf_op jit(solution)/shard_map/all_to_all | solution.py:176
  113.0 0.0 copy-done.1
  113.0 0.0 copy-done.2
  113.0 0.9 shard_map.67
  (2 shorter events, 0.0 us)
Async XLA Ops:
  53.0 10.0 %collective-permute-start = (bf16[320,512]{1,0:T(8,128)(2,1)S(1)}, bf16[320,512]{1,0:T(8,128)(2,1)S(1)}, u32[]{:S(2)}, u32[]{:S(2)}) collective-permute-start(bf16[320,512]{1,0:T(8,128)(2,1)S(1)} %slice.8), channel_id=1, source_target_pairs={{0,32},{1,993},{32,64},{33,1},{64,96},{65,33},{96,128},{97,65},{12... | collective-permute-start | bytes 983048 | tf_op jit(solution)/shard_map/ppermute | solution.py:118
  56.5 14.8 %collective-permute-start.4 = (bf16[512,512]{1,0:T(8,128)(2,1)S(1)}, bf16[512,512]{1,0:T(8,128)(2,1)S(1)}, u32[]{:S(2)}, u32[]{:S(2)}) collective-permute-start(bf16[512,512]{1,0:T(8,128)(2,1)S(1)} %all_gather.3.own_ref), channel_id=1, source_target_pairs={{0,992},{1,33},{32,0},{33,65},{64,32},{65,97},{96,64},{97,129},{12... | collective-permute-start | bytes 1572872 | tf_op jit(solution)/shard_map/ppermute | solution.py:118
  58.4 7.2 %collective-permute-start.2 = (bf16[192,512]{1,0:T(8,128)(2,1)S(1)}, bf16[192,512]{1,0:T(8,128)(2,1)S(1)}, u32[]{:S(2)}, u32[]{:S(2)}) collective-permute-start(bf16[192,512]{1,0:T(8,128)(2,1)S(1)} %slice.9), channel_id=1, source_target_pairs={{0,32},{1,993},{32,64},{33,1},{64,96},{65,33},{96,128},{97,65},{12... | collective-permute-start | bytes 589832 | tf_op jit(solution)/shard_map/ppermute | solution.py:118
  63.0 14.0 %collective-permute-start.1 = (bf16[320,512]{1,0:T(8,128)(2,1)S(1)}, bf16[320,512]{1,0:T(8,128)(2,1)S(1)}, u32[]{:S(2)}, u32[]{:S(2)}) collective-permute-start(bf16[320,512]{1,0:T(8,128)(2,1)S(1)} %collective-permute-done.first_low_ref), channel_id=1, source_target_pairs={{0,32},{1,993},{32,64},{33,1},{64,96},{65,33},{96,128},{97,65},{12... | collective-permute-start | bytes 983048 | tf_op jit(solution)/shard_map/ppermute | solution.py:118
  65.7 11.3 %collective-permute-start.3 = (bf16[192,512]{1,0:T(8,128)(2,1)S(1)}, bf16[192,512]{1,0:T(8,128)(2,1)S(1)}, u32[]{:S(2)}, u32[]{:S(2)}) collective-permute-start(bf16[192,512]{1,0:T(8,128)(2,1)S(1)} %collective-permute-done.2.first_high_ref), channel_id=1, source_target_pairs={{0,32},{1,993},{32,64},{33,1},{64,96},{65,33},{96,128},{97,65},{12... | collective-permute-start | bytes 589832 | tf_op jit(solution)/shard_map/ppermute | solution.py:118
  71.3 1.0 copy-start
  72.3 0.7 copy-start.3
  78.3 12.7 %collective-permute-start.5 = (bf16[16,64,512]{2,1,0:T(8,128)(2,1)S(1)}, bf16[16,64,512]{2,1,0:T(8,128)(2,1)S(1)}, u32[]{:S(2)}, u32[]{:S(2)}) collective-permute-start(bf16[16,64,512]{2,1,0:T(8,128)(2,1)S(1)} %get-tuple-element.8), channel_id=1, source_target_pairs={{0,1},{1,0},{2,3},{3,2},{4,5},{5,4},{6,7},{7,6},{8,9},{9,8},{10,11... | collective-permute-start | bytes 3145736 | tf_op jit(solution)/shard_map/ppermute | solution.py:168
  91.0 22.0 %copy-start.1 = (bf16[512,512]{1,0:T(8,128)(2,1)S(1)}, bf16[512,512]{1,0:T(8,128)(2,1)}, u32[]{:S(2)}) copy-start(bf16[512,512]{1,0:T(8,128)(2,1)} %weight_ref.1) | copy-start | bytes 1572868
  91.0 22.0 %copy-start.2 = (f32[512]{0:T(512)S(1)}, f32[512]{0:T(512)}, u32[]{:S(2)}) copy-start(f32[512]{0:T(512)} %param.11) | copy-start | bytes 6148

commit v6 on v5

--- a/solution.py
+++ b/solution.py
@@ -11,10 +11,10 @@
 VMEM_LIMIT = 16 * 1024 * 1024
 
 
-def each_live(index_ref, count_ref, slots, send_blocks, work):
+def each_slot(places, count, slots, send_blocks, work):
     for s in range(slots):
-        place_in_tile = index_ref[0, 0, s]
-        pl.when(s < count_ref[0, 0])(
+        place_in_tile = places(s)
+        pl.when(s < count)(
             lambda s=s, e=place_in_tile: work(
                 s, lax.div(e, send_blocks), lax.rem(e, send_blocks)
             )
@@ -22,11 +22,17 @@
 
 
 def near_kernel(
-    index_ref, count_ref, values_ref, own_ref, first_low_ref, first_high_ref, second_ref,
-    total_ref, panel,
+    count_ref, values_ref, index_ref, own_ref, first_low_ref, first_high_ref, second_ref,
+    total_ref, kept_ref, places, panel, values_sem, index_sem,
 ):
+    fetches = (
+        pltpu.make_async_copy(values_ref, kept_ref, values_sem),
+        pltpu.make_async_copy(index_ref, places, index_sem),
+    )
+    for fetch in fetches:
+        fetch.start()
     place, core = lax.axis_index("zi"), lax.axis_index("core")
-    slots, side = values_ref.shape[2], values_ref.shape[3]
+    slots, side = kept_ref.shape[2], kept_ref.shape[3]
     shard = panel.shape[0] // lax.axis_size("zo") // STRIDE
     classes = lax.axis_size("zo")
     send_blocks = panel.shape[0] // side
@@ -43,19 +49,21 @@
             else:
                 panel[rows, :] = jnp.zeros((shard, panel.shape[1]), panel.dtype)
     total_ref[...] = jnp.zeros_like(total_ref)
+    for fetch in fetches:
+        fetch.wait()
 
     def work(s, block_row, block_col):
         rows = pl.ds(pl.multiple_of(block_row * side, side), side)
         nodes = pl.ds(pl.multiple_of(block_col * side, side), side)
         total_ref[rows, :] += jnp.dot(
-            values_ref[0, 0, s], panel[nodes, :], preferred_element_type=jnp.float32
-        )
-
-    each_live(index_ref, count_ref, slots, send_blocks, work)
+            kept_ref[0, 0, s], panel[nodes, :], preferred_element_type=jnp.float32
+        )
+
+    each_slot(lambda s: places[0, 0, s], count_ref[0, 0], slots, send_blocks, work)
 
 
 def far_kernel(
-    index_ref, count_ref, values_ref, far_low_ref, far_high_ref, total_in_ref,
+    values_ref, index_ref, count_ref, far_low_ref, far_high_ref, total_in_ref,
     total_ref, theirs_ref, far,
 ):
     del total_in_ref
@@ -86,7 +94,9 @@
 
         @pl.when(lax.rem(far_class, per_block) == part)
         def _():
-            each_live(index_ref, count_ref, slots, send_blocks, work)
+            each_slot(
+                lambda s: index_ref[0, 0, s], count_ref[0, 0], slots, send_blocks, work
+            )
 
     for d in range(dests):
         row = pl.multiple_of((2 * d + 1 - core) * shard, shard)
@@ -146,25 +156,39 @@
             transcendentals=0,
         )
 
-    total = pl.pallas_call(
+    tile = (block_values, block_index)
+    total, *kept = pl.pallas_call(
         near_kernel,
-        out_shape=sums,
-        in_specs=[smem, smem] + [vmem] * 5,
-        out_specs=vmem,
-        scratch_shapes=[pltpu.VMEM((z_size * shard, feat), jnp.bfloat16)],
+        out_shape=(
+            sums,
+            *(jax.ShapeDtypeStruct(a.shape, a.dtype) for a in tile),
+        ),
+        in_specs=[smem] + [pl.BlockSpec(memory_space=pltpu.HBM)] * 2 + [vmem] * 4,
+        out_specs=(vmem, vmem, smem),
+        scratch_shapes=[
+            pltpu.VMEM((z_size * shard, feat), jnp.bfloat16),
+            pltpu.SemaphoreType.DMA,
+            pltpu.SemaphoreType.DMA,
+        ],
         compiler_params=params,
         cost_estimate=cost(0.75),
-    )(block_index, block_count, block_values, own, *first, second)
+    )(
+        block_count,
+        *(pltpu.with_memory_space_constraint(array, pltpu.HBM) for array in tile),
+        own,
+        *first,
+        second,
+    )
     total, theirs = pl.pallas_call(
         far_kernel,
         out_shape=(sums, half_sums),
-        in_specs=[smem, smem] + [vmem] * 4,
+        in_specs=[vmem, smem, smem] + [vmem] * 3,
         out_specs=(vmem, vmem),
         input_output_aliases={5: 0},
         scratch_shapes=[pltpu.VMEM(own.shape, own.dtype)],
         compiler_params=params,
         cost_estimate=cost(0.25),
-    )(block_index, block_count, block_values, *far, total)
+    )(*kept, block_count, *far, total)
     sibling = lax.ppermute(theirs, "core", [(0, 1), (1, 0)])
     both = pl.pallas_call(
         pair_kernel,

time: 114 us -> 115 us (level)
  Pallas kernels: 4.58 us -> 7.49 us
  local copies, waits for them, and re-layouts: 1.74 us -> 0.04 us
    pallas_call x2, Pallas kernels: 3.45 us -> 6.36 us  [the longest x1 4.5 us: local(): pl.pallas_call(near_kernel, out_shape=(sums, *(jax.ShapeDtypeStruct(a.sha...]
    unnamed x8 -> x4, local copies, waits for them, and re-layouts: 1.7 us -> 0.01 us
  transfers between devices with their start and end apart: 6 -> 6, of which waited for: 2 -> 2; matrix products, arithmetic and copies ran while one was open for 0% -> 0% of each run, Pallas kernels for 2% -> 4%
where the time goes in v6:
time: 115 us; the launch traced here: 114 us
  blocking collectives  75.6 us (66%)
  starting transfers between devices  27.1 us (24%)
  Pallas kernels  7.49 us (7%)
  waiting for transfers between devices  3.46 us (3%)
    all_gather x1, blocking collectives, local(): own = lax.all_gather(features, 'zo', axis=0, tiled=True)  53 us
    all_to_all x1, blocking collectives, local(): parts = lax.all_to_all(both, XY, 0, 0, tiled=True)  22.6 us
    ppermute x5, starting transfers between devices, turn(): lax.ppermute(array, Z + ('core',), [(2 * z + c, 2 * ((z + sign * (1 - 2 *...  17.5 us
    ppermute x1, starting transfers between devices, local(): sibling = lax.ppermute(theirs, 'core', [(0, 1), (1, 0)])  9.56 us
    pallas_call x1, Pallas kernels, local(): pl.pallas_call(near_kernel, out_shape=(sums, *(jax.ShapeDtypeStruct(a.sha...  4.5 us
  transfers between devices with their start and end apart: 6, of which 2 were waited for; matrix products, arithmetic and copies ran while one was open for 0% of the time, Pallas kernels for 4%

profile of v6, /device:TPU:1, one launch (start us, length us, event | category | flops | bytes accessed | tf_op | source)
XLA Modules:
  0.0 114.4 jit_solution(8448294363972919133)
XLA Ops:
  0.0 53.0 %all_gather.3.own_ref = bf16[512,512]{1,0:T(8,128)(2,1)S(1)} all-gather(bf16[64,512]{1,0:T(8,128)(2,1)} %param.6), channel_id=1, replica_groups=mesh['zo'=8,'zi'=4,'x'=4,'y'=4,'core'=2] {'zo'}, dimensions={0}, use_global_device_ids=true | all-gather | bytes 589824 | tf_op jit(solution)/shard_map/all_gather | solution.py:138
  53.0 3.5 %collective-permute-start = (bf16[320,512]{1,0:T(8,128)(2,1)S(1)}, bf16[320,512]{1,0:T(8,128)(2,1)S(1)}, u32[]{:S(2)}, u32[]{:S(2)}) collective-permute-start(bf16[320,512]{1,0:T(8,128)(2,1)S(1)} %slice.8), channel_id=1, source_target_pairs={{0,32},{1,993},{32,64},{33,1},{64,96},{65,33},{96,128},{97,65},{12... | collective-permute-start | bytes 983048 | tf_op jit(solution)/shard_map/ppermute | solution.py:128
  56.5 1.9 %collective-permute-start.2 = (bf16[512,512]{1,0:T(8,128)(2,1)S(1)}, bf16[512,512]{1,0:T(8,128)(2,1)S(1)}, u32[]{:S(2)}, u32[]{:S(2)}) collective-permute-start(bf16[512,512]{1,0:T(8,128)(2,1)S(1)} %all_gather.3.own_ref), channel_id=1, source_target_pairs={{0,992},{1,33},{32,0},{33,65},{64,32},{65,97},{96,64},{97,129},{12... | collective-permute-start | bytes 1572872 | tf_op jit(solution)/shard_map/ppermute | solution.py:128
  58.4 4.6 %collective-permute-start.1 = (bf16[192,512]{1,0:T(8,128)(2,1)S(1)}, bf16[192,512]{1,0:T(8,128)(2,1)S(1)}, u32[]{:S(2)}, u32[]{:S(2)}) collective-permute-start(bf16[192,512]{1,0:T(8,128)(2,1)S(1)} %slice.9), channel_id=1, source_target_pairs={{0,32},{1,993},{32,64},{33,1},{64,96},{65,33},{96,128},{97,65},{12... | collective-permute-start | bytes 589832 | tf_op jit(solution)/shard_map/ppermute | solution.py:128
  63.0 0.0 collective-permute-done.first_low_ref
  63.0 2.6 %collective-permute-start.3 = (bf16[320,512]{1,0:T(8,128)(2,1)S(1)}, bf16[320,512]{1,0:T(8,128)(2,1)S(1)}, u32[]{:S(2)}, u32[]{:S(2)}) collective-permute-start(bf16[320,512]{1,0:T(8,128)(2,1)S(1)} %collective-permute-done.first_low_ref), channel_id=1, source_target_pairs={{0,32},{1,993},{32,64},{33,1},{64,96},{65,33},{96,128},{97,65},{12... | collective-permute-start | bytes 983048 | tf_op jit(solution)/shard_map/ppermute | solution.py:128
  65.7 0.0 collective-permute-done.1.first_high_ref
  65.7 4.9 %collective-permute-start.4 = (bf16[192,512]{1,0:T(8,128)(2,1)S(1)}, bf16[192,512]{1,0:T(8,128)(2,1)S(1)}, u32[]{:S(2)}, u32[]{:S(2)}) collective-permute-start(bf16[192,512]{1,0:T(8,128)(2,1)S(1)} %collective-permute-done.1.first_high_ref), channel_id=1, source_target_pairs={{0,32},{1,993},{32,64},{33,1},{64,96},{65,33},{96,128},{97,65},{12... | collective-permute-start | bytes 589832 | tf_op jit(solution)/shard_map/ppermute | solution.py:128
  71.3 0.0 collective-permute-done.2.second_ref
  71.3 4.5 %shard_map.64 = (f32[2048,512]{1,0:T(8,128)S(1)}, bf16[1,1,16,128,128]{4,3,2,1,0:T(8,128)(2,1)S(1)}, s32[1,1,16]{2,1,0:T(1,128)S(1)}) custom-call(s32[1,1]{1,0:T(1,128)S(6)} %copy.9.count_ref, bf16[1,1,16,128,128]{4,3,2,1,0:T(8,128)(2,1)} %values_ref.1, s32[1,1,16]{2,1,0:T(1,128)} %index_ref.1, bf16[512,512]{1,0:T(8,128)(2,1)S(1)} %all_gather.3.own_ref, ...), custom_call_target="tpu_custom_call" | custom-call | flops 201326592 | bytes 6291456 | tf_op jit(solution)/shard_map/pallas_call | solution.py:160
  75.8 1.2 %collective-permute-done.4.far_high_ref = bf16[192,512]{1,0:T(8,128)(2,1)S(1)} collective-permute-done((bf16[192,512]{1,0:T(8,128)(2,1)S(1)}, bf16[192,512]{1,0:T(8,128)(2,1)S(1)}, u32[]{:S(2)}, u32[]{:S(2)}) %collective-permute-start.4) | collective-permute-done | bytes 196640 | tf_op jit(solution)/shard_map/ppermute | solution.py:128
  77.0 0.0 collective-permute-done.3.far_low_ref
  77.0 1.9 %shard_map.65 = (f32[2048,512]{1,0:T(8,128)S(1)}, bf16[16,64,512]{2,1,0:T(8,128)(2,1)S(1)}) custom-call(bf16[1,1,16,128,128]{4,3,2,1,0:T(8,128)(2,1)S(1)} %get-tuple-element.10.values_ref, s32[1,1,16]{2,1,0:T(1,128)S(1)} %get-tuple-element.11.index_ref, s32[1,1]{1,0:T(1,128)S(6)} %copy.9.count_ref, ...), custom_call_target="tpu_custom_call", output_to_operand_aliasing={{0}: (5, {})} | custom-call | flops 67108864 | bytes 2097152 | tf_op jit(solution)/shard_map/pallas_call | solution.py:182
  78.8 9.6 %collective-permute-start.5 = (bf16[16,64,512]{2,1,0:T(8,128)(2,1)S(1)}, bf16[16,64,512]{2,1,0:T(8,128)(2,1)S(1)}, u32[]{:S(2)}, u32[]{:S(2)}) collective-permute-start(bf16[16,64,512]{2,1,0:T(8,128)(2,1)S(1)} %get-tuple-element.14), channel_id=1, source_target_pairs={{0,1},{1,0},{2,3},{3,2},{4,5},{5,4},{6,7},{7,6},{8,9},{9,8},{10,11... | collective-permute-start | bytes 3145736 | tf_op jit(solution)/shard_map/ppermute | solution.py:192
  88.4 2.3 %collective-permute-done.5.sibling_ref = bf16[16,64,512]{2,1,0:T(8,128)(2,1)S(1)} collective-permute-done((bf16[16,64,512]{2,1,0:T(8,128)(2,1)S(1)}, bf16[16,64,512]{2,1,0:T(8,128)(2,1)S(1)}, u32[]{:S(2)}, u32[]{:S(2)}) %collective-permute-start.5) | collective-permute-done | bytes 1048608 | tf_op jit(solution)/shard_map/ppermute | solution.py:192
  90.7 0.0 copy-start
  90.7 0.0 copy-start.1
  90.7 0.2 shard_map.66
  90.9 22.6 %all_to_all.5.parts_ref = bf16[16,64,512]{2,1,0:T(8,128)(2,1)S(1)} all-to-all(bf16[16,64,512]{2,1,0:T(8,128)(2,1)S(1)} %shard_map.66), channel_id=1, replica_groups=mesh['zo'=8,'zi'=4,'x'=4,'y'=4,'core'=2] {'x','y'}, dimensions={0} | all-to-all | bytes 2097152 | tf_op jit(solution)/shard_map/all_to_all | solution.py:200
  113.5 0.0 copy-done
  113.5 0.0 copy-done.1
  113.5 0.9 shard_map.67
  (2 shorter events, 0.0 us)
Async XLA Ops:
  53.0 10.0 %collective-permute-start = (bf16[320,512]{1,0:T(8,128)(2,1)S(1)}, bf16[320,512]{1,0:T(8,128)(2,1)S(1)}, u32[]{:S(2)}, u32[]{:S(2)}) collective-permute-start(bf16[320,512]{1,0:T(8,128)(2,1)S(1)} %slice.8), channel_id=1, source_target_pairs={{0,32},{1,993},{32,64},{33,1},{64,96},{65,33},{96,128},{97,65},{12... | collective-permute-start | bytes 983048 | tf_op jit(solution)/shard_map/ppermute | solution.py:128
  56.5 14.8 %collective-permute-start.2 = (bf16[512,512]{1,0:T(8,128)(2,1)S(1)}, bf16[512,512]{1,0:T(8,128)(2,1)S(1)}, u32[]{:S(2)}, u32[]{:S(2)}) collective-permute-start(bf16[512,512]{1,0:T(8,128)(2,1)S(1)} %all_gather.3.own_ref), channel_id=1, source_target_pairs={{0,992},{1,33},{32,0},{33,65},{64,32},{65,97},{96,64},{97,129},{12... | collective-permute-start | bytes 1572872 | tf_op jit(solution)/shard_map/ppermute | solution.py:128
  58.4 7.2 %collective-permute-start.1 = (bf16[192,512]{1,0:T(8,128)(2,1)S(1)}, bf16[192,512]{1,0:T(8,128)(2,1)S(1)}, u32[]{:S(2)}, u32[]{:S(2)}) collective-permute-start(bf16[192,512]{1,0:T(8,128)(2,1)S(1)} %slice.9), channel_id=1, source_target_pairs={{0,32},{1,993},{32,64},{33,1},{64,96},{65,33},{96,128},{97,65},{12... | collective-permute-start | bytes 589832 | tf_op jit(solution)/shard_map/ppermute | solution.py:128
  63.0 14.0 %collective-permute-start.3 = (bf16[320,512]{1,0:T(8,128)(2,1)S(1)}, bf16[320,512]{1,0:T(8,128)(2,1)S(1)}, u32[]{:S(2)}, u32[]{:S(2)}) collective-permute-start(bf16[320,512]{1,0:T(8,128)(2,1)S(1)} %collective-permute-done.first_low_ref), channel_id=1, source_target_pairs={{0,32},{1,993},{32,64},{33,1},{64,96},{65,33},{96,128},{97,65},{12... | collective-permute-start | bytes 983048 | tf_op jit(solution)/shard_map/ppermute | solution.py:128
  65.7 11.3 %collective-permute-start.4 = (bf16[192,512]{1,0:T(8,128)(2,1)S(1)}, bf16[192,512]{1,0:T(8,128)(2,1)S(1)}, u32[]{:S(2)}, u32[]{:S(2)}) collective-permute-start(bf16[192,512]{1,0:T(8,128)(2,1)S(1)} %collective-permute-done.1.first_high_ref), channel_id=1, source_target_pairs={{0,32},{1,993},{32,64},{33,1},{64,96},{65,33},{96,128},{97,65},{12... | collective-permute-start | bytes 589832 | tf_op jit(solution)/shard_map/ppermute | solution.py:128
  78.8 11.8 %collective-permute-start.5 = (bf16[16,64,512]{2,1,0:T(8,128)(2,1)S(1)}, bf16[16,64,512]{2,1,0:T(8,128)(2,1)S(1)}, u32[]{:S(2)}, u32[]{:S(2)}) collective-permute-start(bf16[16,64,512]{2,1,0:T(8,128)(2,1)S(1)} %get-tuple-element.14), channel_id=1, source_target_pairs={{0,1},{1,0},{2,3},{3,2},{4,5},{5,4},{6,7},{7,6},{8,9},{9,8},{10,11... | collective-permute-start | bytes 3145736 | tf_op jit(solution)/shard_map/ppermute | solution.py:192
  90.7 22.8 %copy-start = (bf16[512,512]{1,0:T(8,128)(2,1)S(1)}, bf16[512,512]{1,0:T(8,128)(2,1)}, u32[]{:S(2)}) copy-start(bf16[512,512]{1,0:T(8,128)(2,1)} %weight_ref.1) | copy-start | bytes 1572868
  90.7 22.8 %copy-start.1 = (f32[512]{0:T(512)S(1)}, f32[512]{0:T(512)}, u32[]{:S(2)}) copy-start(f32[512]{0:T(512)} %param.11) | copy-start | bytes 6148

commit v7 on v6

--- a/solution.py
+++ b/solution.py
@@ -13,12 +13,8 @@
 
 def each_slot(places, count, slots, send_blocks, work):
     for s in range(slots):
-        place_in_tile = places(s)
-        pl.when(s < count)(
-            lambda s=s, e=place_in_tile: work(
-                s, lax.div(e, send_blocks), lax.rem(e, send_blocks)
-            )
-        )
+        e = places(s)
+        work(s, lax.div(e, send_blocks), lax.rem(e, send_blocks), s < count)
 
 
 def near_kernel(
@@ -52,21 +48,22 @@
     for fetch in fetches:
         fetch.wait()
 
-    def work(s, block_row, block_col):
+    def work(s, block_row, block_col, live):
         rows = pl.ds(pl.multiple_of(block_row * side, side), side)
         nodes = pl.ds(pl.multiple_of(block_col * side, side), side)
+        values = jnp.where(live, kept_ref[0, 0, s], 0)
         total_ref[rows, :] += jnp.dot(
-            kept_ref[0, 0, s], panel[nodes, :], preferred_element_type=jnp.float32
+            values, panel[nodes, :], preferred_element_type=jnp.float32
         )
 
     each_slot(lambda s: places[0, 0, s], count_ref[0, 0], slots, send_blocks, work)
 
 
 def far_kernel(
-    values_ref, index_ref, count_ref, far_low_ref, far_high_ref, total_in_ref,
-    total_ref, theirs_ref, far,
+    values_ref, index_ref, count_ref, far_low_ref, far_high_ref, total_ref,
+    total_out_ref, theirs_ref, mine_ref, far,
 ):
-    del total_in_ref
+    del total_out_ref
     place, core = lax.axis_index("zi"), lax.axis_index("core")
     slots, side = values_ref.shape[2], values_ref.shape[3]
     dests, shard, _ = theirs_ref.shape
@@ -79,18 +76,17 @@
 
     for part in range(per_block):
 
-        def work(s, block_row, block_col, part=part):
+        def work(s, block_row, block_col, live, part=part):
             node = block_col * per_block + part
-
-            @pl.when(lax.rem(node, STRIDE) == far_class)
-            def _():
-                rows = pl.ds(pl.multiple_of(block_row * side, side), side)
-                nodes = pl.ds(pl.multiple_of(lax.div(node, STRIDE) * shard, shard), shard)
-                total_ref[rows, :] += jnp.dot(
-                    values_ref[0, 0, s, :, part * shard : (part + 1) * shard],
-                    far[nodes, :],
-                    preferred_element_type=jnp.float32,
-                )
+            match = live & (lax.rem(node, STRIDE) == far_class)
+            rows = pl.ds(pl.multiple_of(block_row * side, side), side)
+            nodes = pl.ds(pl.multiple_of(lax.div(node, STRIDE) * shard, shard), shard)
+            values = values_ref[0, 0, s, :, part * shard : (part + 1) * shard]
+            total_ref[rows, :] += jnp.dot(
+                jnp.where(match, values, 0),
+                far[nodes, :],
+                preferred_element_type=jnp.float32,
+            )
 
         @pl.when(lax.rem(far_class, per_block) == part)
         def _():
@@ -98,18 +94,15 @@
                 lambda s: index_ref[0, 0, s], count_ref[0, 0], slots, send_blocks, work
             )
 
-    for d in range(dests):
-        row = pl.multiple_of((2 * d + 1 - core) * shard, shard)
-        theirs_ref[d] = total_ref[pl.ds(row, shard), :].astype(theirs_ref.dtype)
-
-
-def pair_kernel(total_ref, sibling_ref, out_ref):
-    core = lax.axis_index("core")
-    dests, shard, _ = out_ref.shape
-    for d in range(dests):
-        row = pl.multiple_of((2 * d + core) * shard, shard)
-        mine = total_ref[pl.ds(row, shard), :]
-        out_ref[d] = (mine + sibling_ref[d].astype(jnp.float32)).astype(out_ref.dtype)
+    for ref, who in ((theirs_ref, 1 - core), (mine_ref, core)):
+        for d in range(dests):
+            row = pl.multiple_of((2 * d + who) * shard, shard)
+            ref[d] = total_ref[pl.ds(row, shard), :].astype(ref.dtype)
+
+
+def pair_kernel(mine_ref, sibling_ref, out_ref):
+    both = mine_ref[...] + sibling_ref[...].astype(jnp.float32)
+    out_ref[...] = both.astype(out_ref.dtype)
 
 
 def final_kernel(parts_ref, weight_ref, bias_ref, out_ref):
@@ -179,11 +172,11 @@
         *first,
         second,
     )
-    total, theirs = pl.pallas_call(
+    _, theirs, mine = pl.pallas_call(
         far_kernel,
-        out_shape=(sums, half_sums),
+        out_shape=(sums, half_sums, jax.ShapeDtypeStruct(half_sums.shape, jnp.float32)),
         in_specs=[vmem, smem, smem] + [vmem] * 3,
-        out_specs=(vmem, vmem),
+        out_specs=(vmem, vmem, vmem),
         input_output_aliases={5: 0},
         scratch_shapes=[pltpu.VMEM(own.shape, own.dtype)],
         compiler_params=params,
@@ -196,7 +189,7 @@
         in_specs=[vmem] * 2,
         out_specs=vmem,
         compiler_params=params,
-    )(total, sibling)
+    )(mine, sibling)
     parts = lax.all_to_all(both, XY, 0, 0, tiled=True)
     return pl.pallas_call(
         final_kernel,

time: 115 us -> 114 us (level)
  Pallas kernels: 7.49 us -> 4.9 us
  waiting for transfers between devices: 3.46 us -> 5.66 us
    ppermute x5, waiting for transfers between devices: 1.2 us -> 3.39 us  [turn(): lax.ppermute(array, Z + ('core',), [(2 * z + c, 2 * ((z + sign * (1 - 2 *...]
    pallas_call x1, Pallas kernels: 4.5 us -> 2.3 us  [local(): pl.pallas_call(near_kernel, out_shape=(sums, *(jax.ShapeDtypeStruct(a.sha...]
  transfers between devices with their start and end apart: 6 -> 6, of which waited for: 2 -> 2; matrix products, arithmetic and copies ran while one was open for 0% -> 0% of each run, Pallas kernels for 4% -> 2%
where the time goes in v7:
time: 114 us
  blocking collectives  74.9 us (66%)
  starting transfers between devices  27.4 us (24%)
  waiting for transfers between devices  5.66 us (5%)
  Pallas kernels  4.9 us (4%)
    all_gather x1, blocking collectives, local(): own = lax.all_gather(features, 'zo', axis=0, tiled=True)  53 us
    all_to_all x1, blocking collectives, local(): parts = lax.all_to_all(both, XY, 0, 0, tiled=True)  21.9 us
    ppermute x5, starting transfers between devices, turn(): lax.ppermute(array, Z + ('core',), [(2 * z + c, 2 * ((z + sign * (1 - 2 *...  17.5 us
    ppermute x1, starting transfers between devices, local(): sibling = lax.ppermute(theirs, 'core', [(0, 1), (1, 0)])  9.89 us
    ppermute x5, waiting for transfers between devices, turn(): lax.ppermute(array, Z + ('core',), [(2 * z + c, 2 * ((z + sign * (1 - 2 *...  3.39 us
    pallas_call x1, Pallas kernels, local(): pl.pallas_call(near_kernel, out_shape=(sums, *(jax.ShapeDtypeStruct(a.sha...  2.3 us
  transfers between devices with their start and end apart: 6, of which 2 were waited for; matrix products, arithmetic and copies ran while one was open for 0% of the time, Pallas kernels for 2%

profile of v7, /device:TPU:1, one launch (start us, length us, event | category | flops | bytes accessed | tf_op | source)
XLA Modules:
  0.0 113.7 jit_solution(13500510631158347031)
XLA Ops:
  0.0 53.0 %all_gather.3.own_ref = bf16[512,512]{1,0:T(8,128)(2,1)S(1)} all-gather(bf16[64,512]{1,0:T(8,128)(2,1)} %param.6), channel_id=1, replica_groups=mesh['zo'=8,'zi'=4,'x'=4,'y'=4,'core'=2] {'zo'}, dimensions={0}, use_global_device_ids=true | all-gather | bytes 589824 | tf_op jit(solution)/shard_map/all_gather | solution.py:131
  53.0 3.5 %collective-permute-start = (bf16[320,512]{1,0:T(8,128)(2,1)S(1)}, bf16[320,512]{1,0:T(8,128)(2,1)S(1)}, u32[]{:S(2)}, u32[]{:S(2)}) collective-permute-start(bf16[320,512]{1,0:T(8,128)(2,1)S(1)} %slice.8), channel_id=1, source_target_pairs={{0,32},{1,993},{32,64},{33,1},{64,96},{65,33},{96,128},{97,65},{12... | collective-permute-start | bytes 983048 | tf_op jit(solution)/shard_map/ppermute | solution.py:121
  56.5 1.9 %collective-permute-start.2 = (bf16[512,512]{1,0:T(8,128)(2,1)S(1)}, bf16[512,512]{1,0:T(8,128)(2,1)S(1)}, u32[]{:S(2)}, u32[]{:S(2)}) collective-permute-start(bf16[512,512]{1,0:T(8,128)(2,1)S(1)} %all_gather.3.own_ref), channel_id=1, source_target_pairs={{0,992},{1,33},{32,0},{33,65},{64,32},{65,97},{96,64},{97,129},{12... | collective-permute-start | bytes 1572872 | tf_op jit(solution)/shard_map/ppermute | solution.py:121
  58.4 4.6 %collective-permute-start.1 = (bf16[192,512]{1,0:T(8,128)(2,1)S(1)}, bf16[192,512]{1,0:T(8,128)(2,1)S(1)}, u32[]{:S(2)}, u32[]{:S(2)}) collective-permute-start(bf16[192,512]{1,0:T(8,128)(2,1)S(1)} %slice.9), channel_id=1, source_target_pairs={{0,32},{1,993},{32,64},{33,1},{64,96},{65,33},{96,128},{97,65},{12... | collective-permute-start | bytes 589832 | tf_op jit(solution)/shard_map/ppermute | solution.py:121
  63.0 0.0 collective-permute-done.first_low_ref
  63.0 2.6 %collective-permute-start.3 = (bf16[320,512]{1,0:T(8,128)(2,1)S(1)}, bf16[320,512]{1,0:T(8,128)(2,1)S(1)}, u32[]{:S(2)}, u32[]{:S(2)}) collective-permute-start(bf16[320,512]{1,0:T(8,128)(2,1)S(1)} %collective-permute-done.first_low_ref), channel_id=1, source_target_pairs={{0,32},{1,993},{32,64},{33,1},{64,96},{65,33},{96,128},{97,65},{12... | collective-permute-start | bytes 983048 | tf_op jit(solution)/shard_map/ppermute | solution.py:121
  65.7 0.0 collective-permute-done.1.first_high_ref
  65.7 4.9 %collective-permute-start.4 = (bf16[192,512]{1,0:T(8,128)(2,1)S(1)}, bf16[192,512]{1,0:T(8,128)(2,1)S(1)}, u32[]{:S(2)}, u32[]{:S(2)}) collective-permute-start(bf16[192,512]{1,0:T(8,128)(2,1)S(1)} %collective-permute-done.1.first_high_ref), channel_id=1, source_target_pairs={{0,32},{1,993},{32,64},{33,1},{64,96},{65,33},{96,128},{97,65},{12... | collective-permute-start | bytes 589832 | tf_op jit(solution)/shard_map/ppermute | solution.py:121
  71.3 0.0 collective-permute-done.2.second_ref
  71.3 2.3 %shard_map.64 = (f32[2048,512]{1,0:T(8,128)S(1)}, bf16[1,1,16,128,128]{4,3,2,1,0:T(8,128)(2,1)S(1)}, s32[1,1,16]{2,1,0:T(1,128)S(1)}) custom-call(s32[1,1]{1,0:T(1,128)S(6)} %copy.9.count_ref, bf16[1,1,16,128,128]{4,3,2,1,0:T(8,128)(2,1)} %values_ref.1, s32[1,1,16]{2,1,0:T(1,128)} %index_ref.1, bf16[512,512]{1,0:T(8,128)(2,1)S(1)} %all_gather.3.own_ref, ...), custom_call_target="tpu_custom_call" | custom-call | flops 201326592 | bytes 6291456 | tf_op jit(solution)/shard_map/pallas_call | solution.py:153
  73.6 3.4 %collective-permute-done.4.far_high_ref = bf16[192,512]{1,0:T(8,128)(2,1)S(1)} collective-permute-done((bf16[192,512]{1,0:T(8,128)(2,1)S(1)}, bf16[192,512]{1,0:T(8,128)(2,1)S(1)}, u32[]{:S(2)}, u32[]{:S(2)}) %collective-permute-start.4) | collective-permute-done | bytes 196640 | tf_op jit(solution)/shard_map/ppermute | solution.py:121
  77.0 0.0 collective-permute-done.3.far_low_ref
  77.0 1.5 %shard_map.65 = (f32[2048,512]{1,0:T(8,128)S(1)}, bf16[16,64,512]{2,1,0:T(8,128)(2,1)S(1)}, f32[16,64,512]{2,1,0:T(8,128)S(1)}) custom-call(bf16[1,1,16,128,128]{4,3,2,1,0:T(8,128)(2,1)S(1)} %get-tuple-element.10.values_ref, s32[1,1,16]{2,1,0:T(1,128)S(1)} %get-tuple-element.11.index_ref, ...), custom_call_target="tpu_custom_call", output_to_operand_aliasing={{0}: (5, {})} | custom-call | flops 67108864 | bytes 2097152 | tf_op jit(solution)/shard_map/pallas_call | solution.py:175
  78.5 0.0 copy-start
  78.5 0.0 copy-start.1
  78.5 9.9 %collective-permute-start.5 = (bf16[16,64,512]{2,1,0:T(8,128)(2,1)S(1)}, bf16[16,64,512]{2,1,0:T(8,128)(2,1)S(1)}, u32[]{:S(2)}, u32[]{:S(2)}) collective-permute-start(bf16[16,64,512]{2,1,0:T(8,128)(2,1)S(1)} %get-tuple-element.14), channel_id=1, source_target_pairs={{0,1},{1,0},{2,3},{3,2},{4,5},{5,4},{6,7},{7,6},{8,9},{9,8},{10,11... | collective-permute-start | bytes 3145736 | tf_op jit(solution)/shard_map/ppermute | solution.py:185
  88.4 2.3 %collective-permute-done.5.sibling_ref = bf16[16,64,512]{2,1,0:T(8,128)(2,1)S(1)} collective-permute-done((bf16[16,64,512]{2,1,0:T(8,128)(2,1)S(1)}, bf16[16,64,512]{2,1,0:T(8,128)(2,1)S(1)}, u32[]{:S(2)}, u32[]{:S(2)}) %collective-permute-start.5) | collective-permute-done | bytes 1048608 | tf_op jit(solution)/shard_map/ppermute | solution.py:185
  90.7 0.2 shard_map.66
  90.9 21.9 %all_to_all.5.parts_ref = bf16[16,64,512]{2,1,0:T(8,128)(2,1)S(1)} all-to-all(bf16[16,64,512]{2,1,0:T(8,128)(2,1)S(1)} %shard_map.66), channel_id=1, replica_groups=mesh['zo'=8,'zi'=4,'x'=4,'y'=4,'core'=2] {'x','y'}, dimensions={0} | all-to-all | bytes 2097152 | tf_op jit(solution)/shard_map/all_to_all | solution.py:193
  112.8 0.0 copy-done
  112.8 0.0 copy-done.1
  112.8 0.9 shard_map.67
  (2 shorter events, 0.0 us)
Async XLA Ops:
  53.0 10.0 %collective-permute-start = (bf16[320,512]{1,0:T(8,128)(2,1)S(1)}, bf16[320,512]{1,0:T(8,128)(2,1)S(1)}, u32[]{:S(2)}, u32[]{:S(2)}) collective-permute-start(bf16[320,512]{1,0:T(8,128)(2,1)S(1)} %slice.8), channel_id=1, source_target_pairs={{0,32},{1,993},{32,64},{33,1},{64,96},{65,33},{96,128},{97,65},{12... | collective-permute-start | bytes 983048 | tf_op jit(solution)/shard_map/ppermute | solution.py:121
  56.5 14.8 %collective-permute-start.2 = (bf16[512,512]{1,0:T(8,128)(2,1)S(1)}, bf16[512,512]{1,0:T(8,128)(2,1)S(1)}, u32[]{:S(2)}, u32[]{:S(2)}) collective-permute-start(bf16[512,512]{1,0:T(8,128)(2,1)S(1)} %all_gather.3.own_ref), channel_id=1, source_target_pairs={{0,992},{1,33},{32,0},{33,65},{64,32},{65,97},{96,64},{97,129},{12... | collective-permute-start | bytes 1572872 | tf_op jit(solution)/shard_map/ppermute | solution.py:121
  58.4 7.2 %collective-permute-start.1 = (bf16[192,512]{1,0:T(8,128)(2,1)S(1)}, bf16[192,512]{1,0:T(8,128)(2,1)S(1)}, u32[]{:S(2)}, u32[]{:S(2)}) collective-permute-start(bf16[192,512]{1,0:T(8,128)(2,1)S(1)} %slice.9), channel_id=1, source_target_pairs={{0,32},{1,993},{32,64},{33,1},{64,96},{65,33},{96,128},{97,65},{12... | collective-permute-start | bytes 589832 | tf_op jit(solution)/shard_map/ppermute | solution.py:121
  63.0 14.0 %collective-permute-start.3 = (bf16[320,512]{1,0:T(8,128)(2,1)S(1)}, bf16[320,512]{1,0:T(8,128)(2,1)S(1)}, u32[]{:S(2)}, u32[]{:S(2)}) collective-permute-start(bf16[320,512]{1,0:T(8,128)(2,1)S(1)} %collective-permute-done.first_low_ref), channel_id=1, source_target_pairs={{0,32},{1,993},{32,64},{33,1},{64,96},{65,33},{96,128},{97,65},{12... | collective-permute-start | bytes 983048 | tf_op jit(solution)/shard_map/ppermute | solution.py:121
  65.7 11.3 %collective-permute-start.4 = (bf16[192,512]{1,0:T(8,128)(2,1)S(1)}, bf16[192,512]{1,0:T(8,128)(2,1)S(1)}, u32[]{:S(2)}, u32[]{:S(2)}) collective-permute-start(bf16[192,512]{1,0:T(8,128)(2,1)S(1)} %collective-permute-done.1.first_high_ref), channel_id=1, source_target_pairs={{0,32},{1,993},{32,64},{33,1},{64,96},{65,33},{96,128},{97,65},{12... | collective-permute-start | bytes 589832 | tf_op jit(solution)/shard_map/ppermute | solution.py:121
  78.5 34.3 %copy-start = (bf16[512,512]{1,0:T(8,128)(2,1)S(1)}, bf16[512,512]{1,0:T(8,128)(2,1)}, u32[]{:S(2)}) copy-start(bf16[512,512]{1,0:T(8,128)(2,1)} %weight_ref.1) | copy-start | bytes 1572868
  78.5 34.3 %copy-start.1 = (f32[512]{0:T(512)S(1)}, f32[512]{0:T(512)}, u32[]{:S(2)}) copy-start(f32[512]{0:T(512)} %param.11) | copy-start | bytes 6148
  78.5 12.2 %collective-permute-start.5 = (bf16[16,64,512]{2,1,0:T(8,128)(2,1)S(1)}, bf16[16,64,512]{2,1,0:T(8,128)(2,1)S(1)}, u32[]{:S(2)}, u32[]{:S(2)}) collective-permute-start(bf16[16,64,512]{2,1,0:T(8,128)(2,1)S(1)} %get-tuple-element.14), channel_id=1, source_target_pairs={{0,1},{1,0},{2,3},{3,2},{4,5},{5,4},{6,7},{7,6},{8,9},{9,8},{10,11... | collective-permute-start | bytes 3145736 | tf_op jit(solution)/shard_map/ppermute | solution.py:185

commit v8 on v7

--- a/solution.py
+++ b/solution.py
@@ -18,7 +18,7 @@
 
 
 def near_kernel(
-    count_ref, values_ref, index_ref, own_ref, first_low_ref, first_high_ref, second_ref,
+    count_ref, values_ref, index_ref, own_ref, first_low_ref, first_high_ref,
     total_ref, kept_ref, places, panel, values_sem, index_sem,
 ):
     fetches = (
@@ -34,7 +34,7 @@
     send_blocks = panel.shape[0] // side
 
     steps = (0, STRIDE - 1 - 2 * core, 1 + 2 * core, 2)
-    sources = ((own_ref,), (first_low_ref, first_high_ref), (second_ref,), ())
+    sources = ((own_ref,), (first_low_ref, first_high_ref), (), ())
     for step, refs in zip(steps, sources):
         start = lax.rem(place + step, STRIDE)
         shards = [r[k : k + shard, :] for r in refs for k in range(0, r.shape[0], shard)]
@@ -60,7 +60,7 @@
 
 
 def far_kernel(
-    values_ref, index_ref, count_ref, far_low_ref, far_high_ref, total_ref,
+    values_ref, index_ref, count_ref, second_ref, far_low_ref, far_high_ref, total_ref,
     total_out_ref, theirs_ref, mine_ref, far,
 ):
     del total_out_ref
@@ -71,29 +71,31 @@
     half = far_low_ref.shape[0]
     far[:half, :] = far_low_ref[...]
     far[half:, :] = far_high_ref[...]
-    far_class = lax.rem(place + 2, STRIDE)
     per_block = side // shard
 
-    for part in range(per_block):
-
-        def work(s, block_row, block_col, live, part=part):
-            node = block_col * per_block + part
-            match = live & (lax.rem(node, STRIDE) == far_class)
-            rows = pl.ds(pl.multiple_of(block_row * side, side), side)
-            nodes = pl.ds(pl.multiple_of(lax.div(node, STRIDE) * shard, shard), shard)
-            values = values_ref[0, 0, s, :, part * shard : (part + 1) * shard]
-            total_ref[rows, :] += jnp.dot(
-                jnp.where(match, values, 0),
-                far[nodes, :],
-                preferred_element_type=jnp.float32,
-            )
-
-        @pl.when(lax.rem(far_class, per_block) == part)
-        def _():
-            each_slot(
-                lambda s: index_ref[0, 0, s], count_ref[0, 0], slots, send_blocks, work
-            )
-
+    def add_class(shards, group):
+        for part in range(per_block):
+
+            def work(s, block_row, block_col, live, part=part):
+                node = block_col * per_block + part
+                match = live & (lax.rem(node, STRIDE) == group)
+                rows = pl.ds(pl.multiple_of(block_row * side, side), side)
+                nodes = pl.ds(pl.multiple_of(lax.div(node, STRIDE) * shard, shard), shard)
+                values = values_ref[0, 0, s, :, part * shard : (part + 1) * shard]
+                total_ref[rows, :] += jnp.dot(
+                    jnp.where(match, values, 0),
+                    shards[nodes, :],
+                    preferred_element_type=jnp.float32,
+                )
+
+            @pl.when(lax.rem(group, per_block) == part)
+            def _():
+                each_slot(
+                    lambda s: index_ref[0, 0, s], count_ref[0, 0], slots, send_blocks, work
+                )
+
+    add_class(second_ref, lax.rem(place + 1 + 2 * core, STRIDE))
+    add_class(far, lax.rem(place + 2, STRIDE))
     for ref, who in ((theirs_ref, 1 - core), (mine_ref, core)):
         for d in range(dests):
             row = pl.multiple_of((2 * d + who) * shard, shard)
@@ -129,7 +131,7 @@
         )
 
     own = lax.all_gather(features, "zo", axis=0, tiled=True)
-    cut = (lax.axis_size("zo") * 5 // 8) * shard
+    cut = lax.axis_size("zo") // 2 * shard
     first = [turn(own[:cut], 1), turn(own[cut:], 1)]
     second = turn(own, -1)
     far = [turn(part, 1) for part in first]
@@ -156,7 +158,7 @@
             sums,
             *(jax.ShapeDtypeStruct(a.shape, a.dtype) for a in tile),
         ),
-        in_specs=[smem] + [pl.BlockSpec(memory_space=pltpu.HBM)] * 2 + [vmem] * 4,
+        in_specs=[smem] + [pl.BlockSpec(memory_space=pltpu.HBM)] * 2 + [vmem] * 3,
         out_specs=(vmem, vmem, smem),
         scratch_shapes=[
             pltpu.VMEM((z_size * shard, feat), jnp.bfloat16),
@@ -164,24 +166,23 @@
             pltpu.SemaphoreType.DMA,
         ],
         compiler_params=params,
-        cost_estimate=cost(0.75),
+        cost_estimate=cost(0.5),
     )(
         block_count,
         *(pltpu.with_memory_space_constraint(array, pltpu.HBM) for array in tile),
         own,
         *first,
-        second,
     )
     _, theirs, mine = pl.pallas_call(
         far_kernel,
         out_shape=(sums, half_sums, jax.ShapeDtypeStruct(half_sums.shape, jnp.float32)),
-        in_specs=[vmem, smem, smem] + [vmem] * 3,
+        in_specs=[vmem, smem, smem] + [vmem] * 4,
         out_specs=(vmem, vmem, vmem),
-        input_output_aliases={5: 0},
+        input_output_aliases={6: 0},
         scratch_shapes=[pltpu.VMEM(own.shape, own.dtype)],
         compiler_params=params,
-        cost_estimate=cost(0.25),
-    )(*kept, block_count, *far, total)
+        cost_estimate=cost(0.5),
+    )(*kept, block_count, second, *far, total)
     sibling = lax.ppermute(theirs, "core", [(0, 1), (1, 0)])
     both = pl.pallas_call(
         pair_kernel,

time: 114 us -> 116 us (1.018)
  starting transfers between devices: 27.4 us -> 29.3 us
    ppermute x1, starting transfers between devices: 9.89 us -> 13.4 us  [local(): sibling = lax.ppermute(theirs, 'core', [(0, 1), (1, 0)])]
    ppermute x5, starting transfers between devices: 17.5 us -> 15.9 us  [turn(): lax.ppermute(array, Z + ('core',), [(2 * z + c, 2 * ((z + sign * (1 - 2 *...]
where the time goes in v8:
time: 116 us
  blocking collectives  75 us (65%)
  starting transfers between devices  29.3 us (25%)
  Pallas kernels  5.69 us (5%)
  waiting for transfers between devices  4.96 us (4%)
    all_gather x1, blocking collectives, local(): own = lax.all_gather(features, 'zo', axis=0, tiled=True)  53 us
    all_to_all x1, blocking collectives, local(): parts = lax.all_to_all(both, XY, 0, 0, tiled=True)  22 us
    ppermute x5, starting transfers between devices, turn(): lax.ppermute(array, Z + ('core',), [(2 * z + c, 2 * ((z + sign * (1 - 2 *...  15.9 us
    ppermute x1, starting transfers between devices, local(): sibling = lax.ppermute(theirs, 'core', [(0, 1), (1, 0)])  13.4 us
    ppermute x5, waiting for transfers between devices, turn(): lax.ppermute(array, Z + ('core',), [(2 * z + c, 2 * ((z + sign * (1 - 2 *...  2.7 us
  transfers between devices with their start and end apart: 6, of which 2 were waited for; matrix products, arithmetic and copies ran while one was open for 0% of the time, Pallas kernels for 2%

profile of v8, /device:TPU:1, one launch (start us, length us, event | category | flops | bytes accessed | tf_op | source)
XLA Modules:
  0.0 115.7 jit_solution(16268848041606854386)
XLA Ops:
  0.0 53.0 %all_gather.3.own_ref = bf16[512,512]{1,0:T(8,128)(2,1)S(1)} all-gather(bf16[64,512]{1,0:T(8,128)(2,1)} %param.6), channel_id=1, replica_groups=mesh['zo'=8,'zi'=4,'x'=4,'y'=4,'core'=2] {'zo'}, dimensions={0}, use_global_device_ids=true | all-gather | bytes 589824 | tf_op jit(solution)/shard_map/all_gather | solution.py:133
  53.0 3.5 %collective-permute-start.1 = (bf16[256,512]{1,0:T(8,128)(2,1)S(1)}, bf16[256,512]{1,0:T(8,128)(2,1)S(1)}, u32[]{:S(2)}, u32[]{:S(2)}) collective-permute-start(bf16[256,512]{1,0:T(8,128)(2,1)S(1)} %get-tuple-element.15), channel_id=1, source_target_pairs={{0,32},{1,993},{32,64},{33,1},{64,96},{65,33},{96,128},{97,65},{12... | collective-permute-start | bytes 786440 | tf_op jit(solution)/shard_map/ppermute | solution.py:123
  56.5 2.2 %collective-permute-start = (bf16[256,512]{1,0:T(8,128)(2,1)S(1)}, bf16[256,512]{1,0:T(8,128)(2,1)S(1)}, u32[]{:S(2)}, u32[]{:S(2)}) collective-permute-start(bf16[256,512]{1,0:T(8,128)(2,1)S(1)} %get-tuple-element.16), channel_id=1, source_target_pairs={{0,32},{1,993},{32,64},{33,1},{64,96},{65,33},{96,128},{97,65},{12... | collective-permute-start | bytes 786440 | tf_op jit(solution)/shard_map/ppermute | solution.py:123
  58.7 3.1 %collective-permute-start.2 = (bf16[512,512]{1,0:T(8,128)(2,1)S(1)}, bf16[512,512]{1,0:T(8,128)(2,1)S(1)}, u32[]{:S(2)}, u32[]{:S(2)}) collective-permute-start(bf16[512,512]{1,0:T(8,128)(2,1)S(1)} %all_gather.3.own_ref), channel_id=1, source_target_pairs={{0,992},{1,33},{32,0},{33,65},{64,32},{65,97},{96,64},{97,129},{12... | collective-permute-start | bytes 1572872 | tf_op jit(solution)/shard_map/ppermute | solution.py:123
  61.8 0.0 collective-permute-done.1.first_high_ref
  61.8 3.8 %collective-permute-start.4 = (bf16[256,512]{1,0:T(8,128)(2,1)S(1)}, bf16[256,512]{1,0:T(8,128)(2,1)S(1)}, u32[]{:S(2)}, u32[]{:S(2)}) collective-permute-start(bf16[256,512]{1,0:T(8,128)(2,1)S(1)} %collective-permute-done.1.first_high_ref), channel_id=1, source_target_pairs={{0,32},{1,993},{32,64},{33,1},{64,96},{65,33},{96,128},{97,65},{12... | collective-permute-start | bytes 786440 | tf_op jit(solution)/shard_map/ppermute | solution.py:123
  65.6 0.0 collective-permute-done.first_low_ref
  65.6 3.4 %collective-permute-start.3 = (bf16[256,512]{1,0:T(8,128)(2,1)S(1)}, bf16[256,512]{1,0:T(8,128)(2,1)S(1)}, u32[]{:S(2)}, u32[]{:S(2)}) collective-permute-start(bf16[256,512]{1,0:T(8,128)(2,1)S(1)} %collective-permute-done.first_low_ref), channel_id=1, source_target_pairs={{0,32},{1,993},{32,64},{33,1},{64,96},{65,33},{96,128},{97,65},{12... | collective-permute-start | bytes 786440 | tf_op jit(solution)/shard_map/ppermute | solution.py:123
  69.6 2.3 %shard_map.64 = (f32[2048,512]{1,0:T(8,128)S(1)}, bf16[1,1,16,128,128]{4,3,2,1,0:T(8,128)(2,1)S(1)}, s32[1,1,16]{2,1,0:T(1,128)S(1)}) custom-call(s32[1,1]{1,0:T(1,128)S(6)} %copy.9.count_ref, bf16[1,1,16,128,128]{4,3,2,1,0:T(8,128)(2,1)} %values_ref.1, s32[1,1,16]{2,1,0:T(1,128)} %index_ref.1, bf16[512,512]{1,0:T(8,128)(2,1)S(1)} %all_gather.3.own_ref, ...), custom_call_target="tpu_custom_call" | custom-call | flops 134217728 | bytes 4194304 | tf_op jit(solution)/shard_map/pallas_call | solution.py:155
  71.9 0.0 collective-permute-done.4.far_high_ref
  71.9 2.7 %collective-permute-done.3.far_low_ref = bf16[256,512]{1,0:T(8,128)(2,1)S(1)} collective-permute-done((bf16[256,512]{1,0:T(8,128)(2,1)S(1)}, bf16[256,512]{1,0:T(8,128)(2,1)S(1)}, u32[]{:S(2)}, u32[]{:S(2)}) %collective-permute-start.3) | collective-permute-done | bytes 262176 | tf_op jit(solution)/shard_map/ppermute | solution.py:123
  74.6 0.0 collective-permute-done.2.second_ref
  74.6 2.3 %shard_map.65 = (f32[2048,512]{1,0:T(8,128)S(1)}, bf16[16,64,512]{2,1,0:T(8,128)(2,1)S(1)}, f32[16,64,512]{2,1,0:T(8,128)S(1)}) custom-call(bf16[1,1,16,128,128]{4,3,2,1,0:T(8,128)(2,1)S(1)} %get-tuple-element.10.values_ref, s32[1,1,16]{2,1,0:T(1,128)S(1)} %get-tuple-element.11.index_ref, ...), custom_call_target="tpu_custom_call", output_to_operand_aliasing={{0}: (6, {})} | custom-call | flops 134217728 | bytes 4194304 | tf_op jit(solution)/shard_map/pallas_call | solution.py:176
  76.9 0.0 copy-start
  76.9 0.0 copy-start.1
  77.0 13.4 %collective-permute-start.5 = (bf16[16,64,512]{2,1,0:T(8,128)(2,1)S(1)}, bf16[16,64,512]{2,1,0:T(8,128)(2,1)S(1)}, u32[]{:S(2)}, u32[]{:S(2)}) collective-permute-start(bf16[16,64,512]{2,1,0:T(8,128)(2,1)S(1)} %get-tuple-element.14), channel_id=1, source_target_pairs={{0,1},{1,0},{2,3},{3,2},{4,5},{5,4},{6,7},{7,6},{8,9},{9,8},{10,11... | collective-permute-start | bytes 3145736 | tf_op jit(solution)/shard_map/ppermute | solution.py:186
  90.4 2.3 %collective-permute-done.5.sibling_ref = bf16[16,64,512]{2,1,0:T(8,128)(2,1)S(1)} collective-permute-done((bf16[16,64,512]{2,1,0:T(8,128)(2,1)S(1)}, bf16[16,64,512]{2,1,0:T(8,128)(2,1)S(1)}, u32[]{:S(2)}, u32[]{:S(2)}) %collective-permute-start.5) | collective-permute-done | bytes 1048608 | tf_op jit(solution)/shard_map/ppermute | solution.py:186
  92.6 0.2 shard_map.66
  92.8 22.0 %all_to_all.5.parts_ref = bf16[16,64,512]{2,1,0:T(8,128)(2,1)S(1)} all-to-all(bf16[16,64,512]{2,1,0:T(8,128)(2,1)S(1)} %shard_map.66), channel_id=1, replica_groups=mesh['zo'=8,'zi'=4,'x'=4,'y'=4,'core'=2] {'x','y'}, dimensions={0} | all-to-all | bytes 2097152 | tf_op jit(solution)/shard_map/all_to_all | solution.py:194
  114.8 0.0 copy-done
  114.8 0.0 copy-done.1
  114.8 0.9 shard_map.67
  (1 shorter events, 0.0 us)
Async XLA Ops:
  53.0 8.8 %collective-permute-start.1 = (bf16[256,512]{1,0:T(8,128)(2,1)S(1)}, bf16[256,512]{1,0:T(8,128)(2,1)S(1)}, u32[]{:S(2)}, u32[]{:S(2)}) collective-permute-start(bf16[256,512]{1,0:T(8,128)(2,1)S(1)} %get-tuple-element.15), channel_id=1, source_target_pairs={{0,32},{1,993},{32,64},{33,1},{64,96},{65,33},{96,128},{97,65},{12... | collective-permute-start | bytes 786440 | tf_op jit(solution)/shard_map/ppermute | solution.py:123
  56.5 9.1 %collective-permute-start = (bf16[256,512]{1,0:T(8,128)(2,1)S(1)}, bf16[256,512]{1,0:T(8,128)(2,1)S(1)}, u32[]{:S(2)}, u32[]{:S(2)}) collective-permute-start(bf16[256,512]{1,0:T(8,128)(2,1)S(1)} %get-tuple-element.16), channel_id=1, source_target_pairs={{0,32},{1,993},{32,64},{33,1},{64,96},{65,33},{96,128},{97,65},{12... | collective-permute-start | bytes 786440 | tf_op jit(solution)/shard_map/ppermute | solution.py:123
  58.7 15.9 %collective-permute-start.2 = (bf16[512,512]{1,0:T(8,128)(2,1)S(1)}, bf16[512,512]{1,0:T(8,128)(2,1)S(1)}, u32[]{:S(2)}, u32[]{:S(2)}) collective-permute-start(bf16[512,512]{1,0:T(8,128)(2,1)S(1)} %all_gather.3.own_ref), channel_id=1, source_target_pairs={{0,992},{1,33},{32,0},{33,65},{64,32},{65,97},{96,64},{97,129},{12... | collective-permute-start | bytes 1572872 | tf_op jit(solution)/shard_map/ppermute | solution.py:123
  61.8 10.1 %collective-permute-start.4 = (bf16[256,512]{1,0:T(8,128)(2,1)S(1)}, bf16[256,512]{1,0:T(8,128)(2,1)S(1)}, u32[]{:S(2)}, u32[]{:S(2)}) collective-permute-start(bf16[256,512]{1,0:T(8,128)(2,1)S(1)} %collective-permute-done.1.first_high_ref), channel_id=1, source_target_pairs={{0,32},{1,993},{32,64},{33,1},{64,96},{65,33},{96,128},{97,65},{12... | collective-permute-start | bytes 786440 | tf_op jit(solution)/shard_map/ppermute | solution.py:123
  65.6 9.0 %collective-permute-start.3 = (bf16[256,512]{1,0:T(8,128)(2,1)S(1)}, bf16[256,512]{1,0:T(8,128)(2,1)S(1)}, u32[]{:S(2)}, u32[]{:S(2)}) collective-permute-start(bf16[256,512]{1,0:T(8,128)(2,1)S(1)} %collective-permute-done.first_low_ref), channel_id=1, source_target_pairs={{0,32},{1,993},{32,64},{33,1},{64,96},{65,33},{96,128},{97,65},{12... | collective-permute-start | bytes 786440 | tf_op jit(solution)/shard_map/ppermute | solution.py:123
  76.9 37.9 %copy-start = (bf16[512,512]{1,0:T(8,128)(2,1)S(1)}, bf16[512,512]{1,0:T(8,128)(2,1)}, u32[]{:S(2)}) copy-start(bf16[512,512]{1,0:T(8,128)(2,1)} %weight_ref.1) | copy-start | bytes 1572868
  76.9 37.9 %copy-start.1 = (f32[512]{0:T(512)S(1)}, f32[512]{0:T(512)}, u32[]{:S(2)}) copy-start(f32[512]{0:T(512)} %param.11) | copy-start | bytes 6148
  77.0 15.7 %collective-permute-start.5 = (bf16[16,64,512]{2,1,0:T(8,128)(2,1)S(1)}, bf16[16,64,512]{2,1,0:T(8,128)(2,1)S(1)}, u32[]{:S(2)}, u32[]{:S(2)}) collective-permute-start(bf16[16,64,512]{2,1,0:T(8,128)(2,1)S(1)} %get-tuple-element.14), channel_id=1, source_target_pairs={{0,1},{1,0},{2,3},{3,2},{4,5},{5,4},{6,7},{7,6},{8,9},{9,8},{10,11... | collective-permute-start | bytes 3145736 | tf_op jit(solution)/shard_map/ppermute | solution.py:186

commit v9 on v7

--- a/solution.py
+++ b/solution.py
@@ -129,7 +129,7 @@
         )
 
     own = lax.all_gather(features, "zo", axis=0, tiled=True)
-    cut = (lax.axis_size("zo") * 5 // 8) * shard
+    cut = (lax.axis_size("zo") * 3 // 4) * shard
     first = [turn(own[:cut], 1), turn(own[cut:], 1)]
     second = turn(own, -1)
     far = [turn(part, 1) for part in first]

time: 114 us -> 123 us (1.079)
  waiting for transfers between devices: 5.66 us -> 14.6 us
    ppermute x5, waiting for transfers between devices: 3.39 us -> 12.3 us  [turn(): lax.ppermute(array, Z + ('core',), [(2 * z + c, 2 * ((z + sign * (1 - 2 *...]
  transfers between devices with their start and end apart: 6 -> 6, of which waited for: 2 -> 3; matrix products, arithmetic and copies ran while one was open for 0% -> 0% of each run, Pallas kernels for 2% -> 2%
where the time goes in v9:
time: 123 us; the launch traced here: 122 us
  blocking collectives  75.6 us (61%)
  starting transfers between devices  26.5 us (22%)
  waiting for transfers between devices  14.6 us (12%)
  Pallas kernels  4.9 us (4%)
    all_gather x1, blocking collectives, local(): own = lax.all_gather(features, 'zo', axis=0, tiled=True)  53 us
    all_to_all x1, blocking collectives, local(): parts = lax.all_to_all(both, XY, 0, 0, tiled=True)  22.7 us
    ppermute x5, starting transfers between devices, turn(): lax.ppermute(array, Z + ('core',), [(2 * z + c, 2 * ((z + sign * (1 - 2 *...  17 us
    ppermute x5, waiting for transfers between devices, turn(): lax.ppermute(array, Z + ('core',), [(2 * z + c, 2 * ((z + sign * (1 - 2 *...  12.3 us
    ppermute x1, starting transfers between devices, local(): sibling = lax.ppermute(theirs, 'core', [(0, 1), (1, 0)])  9.58 us
  transfers between devices with their start and end apart: 6, of which 3 were waited for; matrix products, arithmetic and copies ran while one was open for 0% of the time, Pallas kernels for 2%

profile of v9, /device:TPU:1, one launch (start us, length us, event | category | flops | bytes accessed | tf_op | source)
XLA Modules:
  0.0 122.5 jit_solution(9492154651399653785)
XLA Ops:
  0.0 53.0 %all_gather.3.own_ref = bf16[512,512]{1,0:T(8,128)(2,1)S(1)} all-gather(bf16[64,512]{1,0:T(8,128)(2,1)} %param.6), channel_id=1, replica_groups=mesh['zo'=8,'zi'=4,'x'=4,'y'=4,'core'=2] {'zo'}, dimensions={0}, use_global_device_ids=true | all-gather | bytes 589824 | tf_op jit(solution)/shard_map/all_gather | solution.py:131
  53.0 3.5 %collective-permute-start = (bf16[384,512]{1,0:T(8,128)(2,1)S(1)}, bf16[384,512]{1,0:T(8,128)(2,1)S(1)}, u32[]{:S(2)}, u32[]{:S(2)}) collective-permute-start(bf16[384,512]{1,0:T(8,128)(2,1)S(1)} %slice.8), channel_id=1, source_target_pairs={{0,32},{1,993},{32,64},{33,1},{64,96},{65,33},{96,128},{97,65},{12... | collective-permute-start | bytes 1179656 | tf_op jit(solution)/shard_map/ppermute | solution.py:121
  56.5 1.9 %collective-permute-start.2 = (bf16[512,512]{1,0:T(8,128)(2,1)S(1)}, bf16[512,512]{1,0:T(8,128)(2,1)S(1)}, u32[]{:S(2)}, u32[]{:S(2)}) collective-permute-start(bf16[512,512]{1,0:T(8,128)(2,1)S(1)} %all_gather.3.own_ref), channel_id=1, source_target_pairs={{0,992},{1,33},{32,0},{33,65},{64,32},{65,97},{96,64},{97,129},{12... | collective-permute-start | bytes 1572872 | tf_op jit(solution)/shard_map/ppermute | solution.py:121
  58.4 3.6 %collective-permute-done.first_low_ref = bf16[384,512]{1,0:T(8,128)(2,1)S(1)} collective-permute-done((bf16[384,512]{1,0:T(8,128)(2,1)S(1)}, bf16[384,512]{1,0:T(8,128)(2,1)S(1)}, u32[]{:S(2)}, u32[]{:S(2)}) %collective-permute-start) | collective-permute-done | bytes 393248 | tf_op jit(solution)/shard_map/ppermute | solution.py:121
  62.0 4.3 %collective-permute-start.3 = (bf16[384,512]{1,0:T(8,128)(2,1)S(1)}, bf16[384,512]{1,0:T(8,128)(2,1)S(1)}, u32[]{:S(2)}, u32[]{:S(2)}) collective-permute-start(bf16[384,512]{1,0:T(8,128)(2,1)S(1)} %collective-permute-done.first_low_ref), channel_id=1, source_target_pairs={{0,32},{1,993},{32,64},{33,1},{64,96},{65,33},{96,128},{97,65},{12... | collective-permute-start | bytes 1179656 | tf_op jit(solution)/shard_map/ppermute | solution.py:121
  66.4 1.9 %collective-permute-start.1 = (bf16[128,512]{1,0:T(8,128)(2,1)S(1)}, bf16[128,512]{1,0:T(8,128)(2,1)S(1)}, u32[]{:S(2)}, u32[]{:S(2)}) collective-permute-start(bf16[128,512]{1,0:T(8,128)(2,1)S(1)} %slice.9), channel_id=1, source_target_pairs={{0,32},{1,993},{32,64},{33,1},{64,96},{65,33},{96,128},{97,65},{12... | collective-permute-start | bytes 393224 | tf_op jit(solution)/shard_map/ppermute | solution.py:121
  68.3 8.7 %collective-permute-done.1.first_high_ref = bf16[128,512]{1,0:T(8,128)(2,1)S(1)} collective-permute-done((bf16[128,512]{1,0:T(8,128)(2,1)S(1)}, bf16[128,512]{1,0:T(8,128)(2,1)S(1)}, u32[]{:S(2)}, u32[]{:S(2)}) %collective-permute-start.1) | collective-permute-done | bytes 131104 | tf_op jit(solution)/shard_map/ppermute | solution.py:121
  77.0 5.3 %collective-permute-start.4 = (bf16[128,512]{1,0:T(8,128)(2,1)S(1)}, bf16[128,512]{1,0:T(8,128)(2,1)S(1)}, u32[]{:S(2)}, u32[]{:S(2)}) collective-permute-start(bf16[128,512]{1,0:T(8,128)(2,1)S(1)} %collective-permute-done.1.first_high_ref), channel_id=1, source_target_pairs={{0,32},{1,993},{32,64},{33,1},{64,96},{65,33},{96,128},{97,65},{12... | collective-permute-start | bytes 393224 | tf_op jit(solution)/shard_map/ppermute | solution.py:121
  83.0 0.0 collective-permute-done.2.second_ref
  83.0 2.3 %shard_map.64 = (f32[2048,512]{1,0:T(8,128)S(1)}, bf16[1,1,16,128,128]{4,3,2,1,0:T(8,128)(2,1)S(1)}, s32[1,1,16]{2,1,0:T(1,128)S(1)}) custom-call(s32[1,1]{1,0:T(1,128)S(6)} %copy.9.count_ref, bf16[1,1,16,128,128]{4,3,2,1,0:T(8,128)(2,1)} %values_ref.1, s32[1,1,16]{2,1,0:T(1,128)} %index_ref.1, bf16[512,512]{1,0:T(8,128)(2,1)S(1)} %all_gather.3.own_ref, ...), custom_call_target="tpu_custom_call" | custom-call | flops 201326592 | bytes 6291456 | tf_op jit(solution)/shard_map/pallas_call | solution.py:153
  85.3 0.0 collective-permute-done.4.far_high_ref
  85.3 0.0 collective-permute-done.3.far_low_ref
  85.3 1.5 %shard_map.65 = (f32[2048,512]{1,0:T(8,128)S(1)}, bf16[16,64,512]{2,1,0:T(8,128)(2,1)S(1)}, f32[16,64,512]{2,1,0:T(8,128)S(1)}) custom-call(bf16[1,1,16,128,128]{4,3,2,1,0:T(8,128)(2,1)S(1)} %get-tuple-element.10.values_ref, s32[1,1,16]{2,1,0:T(1,128)S(1)} %get-tuple-element.11.index_ref, ...), custom_call_target="tpu_custom_call", output_to_operand_aliasing={{0}: (5, {})} | custom-call | flops 67108864 | bytes 2097152 | tf_op jit(solution)/shard_map/pallas_call | solution.py:175
  86.8 0.0 copy-start
  86.8 0.0 copy-start.1
  86.9 9.6 %collective-permute-start.5 = (bf16[16,64,512]{2,1,0:T(8,128)(2,1)S(1)}, bf16[16,64,512]{2,1,0:T(8,128)(2,1)S(1)}, u32[]{:S(2)}, u32[]{:S(2)}) collective-permute-start(bf16[16,64,512]{2,1,0:T(8,128)(2,1)S(1)} %get-tuple-element.14), channel_id=1, source_target_pairs={{0,1},{1,0},{2,3},{3,2},{4,5},{5,4},{6,7},{7,6},{8,9},{9,8},{10,11... | collective-permute-start | bytes 3145736 | tf_op jit(solution)/shard_map/ppermute | solution.py:185
  96.4 2.3 %collective-permute-done.5.sibling_ref = bf16[16,64,512]{2,1,0:T(8,128)(2,1)S(1)} collective-permute-done((bf16[16,64,512]{2,1,0:T(8,128)(2,1)S(1)}, bf16[16,64,512]{2,1,0:T(8,128)(2,1)S(1)}, u32[]{:S(2)}, u32[]{:S(2)}) %collective-permute-start.5) | collective-permute-done | bytes 1048608 | tf_op jit(solution)/shard_map/ppermute | solution.py:185
  98.7 0.2 shard_map.66
  98.9 22.7 %all_to_all.5.parts_ref = bf16[16,64,512]{2,1,0:T(8,128)(2,1)S(1)} all-to-all(bf16[16,64,512]{2,1,0:T(8,128)(2,1)S(1)} %shard_map.66), channel_id=1, replica_groups=mesh['zo'=8,'zi'=4,'x'=4,'y'=4,'core'=2] {'x','y'}, dimensions={0} | all-to-all | bytes 2097152 | tf_op jit(solution)/shard_map/all_to_all | solution.py:193
  121.6 0.0 copy-done
  121.6 0.0 copy-done.1
  121.6 0.9 shard_map.67
  (2 shorter events, 0.0 us)
Async XLA Ops:
  53.0 9.0 %collective-permute-start = (bf16[384,512]{1,0:T(8,128)(2,1)S(1)}, bf16[384,512]{1,0:T(8,128)(2,1)S(1)}, u32[]{:S(2)}, u32[]{:S(2)}) collective-permute-start(bf16[384,512]{1,0:T(8,128)(2,1)S(1)} %slice.8), channel_id=1, source_target_pairs={{0,32},{1,993},{32,64},{33,1},{64,96},{65,33},{96,128},{97,65},{12... | collective-permute-start | bytes 1179656 | tf_op jit(solution)/shard_map/ppermute | solution.py:121
  56.5 26.5 %collective-permute-start.2 = (bf16[512,512]{1,0:T(8,128)(2,1)S(1)}, bf16[512,512]{1,0:T(8,128)(2,1)S(1)}, u32[]{:S(2)}, u32[]{:S(2)}) collective-permute-start(bf16[512,512]{1,0:T(8,128)(2,1)S(1)} %all_gather.3.own_ref), channel_id=1, source_target_pairs={{0,992},{1,33},{32,0},{33,65},{64,32},{65,97},{96,64},{97,129},{12... | collective-permute-start | bytes 1572872 | tf_op jit(solution)/shard_map/ppermute | solution.py:121
  62.0 23.3 %collective-permute-start.3 = (bf16[384,512]{1,0:T(8,128)(2,1)S(1)}, bf16[384,512]{1,0:T(8,128)(2,1)S(1)}, u32[]{:S(2)}, u32[]{:S(2)}) collective-permute-start(bf16[384,512]{1,0:T(8,128)(2,1)S(1)} %collective-permute-done.first_low_ref), channel_id=1, source_target_pairs={{0,32},{1,993},{32,64},{33,1},{64,96},{65,33},{96,128},{97,65},{12... | collective-permute-start | bytes 1179656 | tf_op jit(solution)/shard_map/ppermute | solution.py:121
  66.4 10.6 %collective-permute-start.1 = (bf16[128,512]{1,0:T(8,128)(2,1)S(1)}, bf16[128,512]{1,0:T(8,128)(2,1)S(1)}, u32[]{:S(2)}, u32[]{:S(2)}) collective-permute-start(bf16[128,512]{1,0:T(8,128)(2,1)S(1)} %slice.9), channel_id=1, source_target_pairs={{0,32},{1,993},{32,64},{33,1},{64,96},{65,33},{96,128},{97,65},{12... | collective-permute-start | bytes 393224 | tf_op jit(solution)/shard_map/ppermute | solution.py:121
  77.0 8.3 %collective-permute-start.4 = (bf16[128,512]{1,0:T(8,128)(2,1)S(1)}, bf16[128,512]{1,0:T(8,128)(2,1)S(1)}, u32[]{:S(2)}, u32[]{:S(2)}) collective-permute-start(bf16[128,512]{1,0:T(8,128)(2,1)S(1)} %collective-permute-done.1.first_high_ref), channel_id=1, source_target_pairs={{0,32},{1,993},{32,64},{33,1},{64,96},{65,33},{96,128},{97,65},{12... | collective-permute-start | bytes 393224 | tf_op jit(solution)/shard_map/ppermute | solution.py:121
  86.8 34.7 %copy-start = (bf16[512,512]{1,0:T(8,128)(2,1)S(1)}, bf16[512,512]{1,0:T(8,128)(2,1)}, u32[]{:S(2)}) copy-start(bf16[512,512]{1,0:T(8,128)(2,1)} %weight_ref.1) | copy-start | bytes 1572868
  86.8 34.7 %copy-start.1 = (f32[512]{0:T(512)S(1)}, f32[512]{0:T(512)}, u32[]{:S(2)}) copy-start(f32[512]{0:T(512)} %param.11) | copy-start | bytes 6148
  86.9 11.9 %collective-permute-start.5 = (bf16[16,64,512]{2,1,0:T(8,128)(2,1)S(1)}, bf16[16,64,512]{2,1,0:T(8,128)(2,1)S(1)}, u32[]{:S(2)}, u32[]{:S(2)}) collective-permute-start(bf16[16,64,512]{2,1,0:T(8,128)(2,1)S(1)} %get-tuple-element.14), channel_id=1, source_target_pairs={{0,1},{1,0},{2,3},{3,2},{4,5},{5,4},{6,7},{7,6},{8,9},{9,8},{10,11... | collective-permute-start | bytes 3145736 | tf_op jit(solution)/shard_map/ppermute | solution.py:185

commit v10 on v7

--- a/solution.py
+++ b/solution.py
@@ -33,7 +33,7 @@
     classes = lax.axis_size("zo")
     send_blocks = panel.shape[0] // side
 
-    steps = (0, STRIDE - 1 - 2 * core, 1 + 2 * core, 2)
+    steps = (0, 1 + 2 * core, STRIDE - 1 - 2 * core, 2)
     sources = ((own_ref,), (first_low_ref, first_high_ref), (second_ref,), ())
     for step, refs in zip(steps, sources):
         start = lax.rem(place + step, STRIDE)
@@ -130,9 +130,9 @@
 
     own = lax.all_gather(features, "zo", axis=0, tiled=True)
     cut = (lax.axis_size("zo") * 5 // 8) * shard
-    first = [turn(own[:cut], 1), turn(own[cut:], 1)]
-    second = turn(own, -1)
-    far = [turn(part, 1) for part in first]
+    first = [turn(own[:cut], -1), turn(own[cut:], -1)]
+    second = turn(own, 1)
+    far = [turn(part, -1) for part in first]
 
     smem = pl.BlockSpec(memory_space=pltpu.SMEM)
     vmem = pl.BlockSpec(memory_space=pltpu.VMEM)

time: 114 us -> 113 us (level)
  starting transfers between devices: 27.4 us -> 19 us
  waiting for transfers between devices: 5.66 us -> 12 us
    ppermute x5, waiting for transfers between devices: 3.39 us -> 9.74 us  [turn(): lax.ppermute(array, Z + ('core',), [(2 * z + c, 2 * ((z + sign * (1 - 2 *...]
    ppermute x5, starting transfers between devices: 17.5 us -> 12.4 us  [turn(): lax.ppermute(array, Z + ('core',), [(2 * z + c, 2 * ((z + sign * (1 - 2 *...]
    ppermute x1, starting transfers between devices: 9.89 us -> 6.59 us  [local(): sibling = lax.ppermute(theirs, 'core', [(0, 1), (1, 0)])]
  transfers between devices with their start and end apart: 6 -> 6, of which waited for: 2 -> 4; matrix products, arithmetic and copies ran while one was open for 0% -> 0% of each run, Pallas kernels for 2% -> 2%
where the time goes in v10:
time: 113 us; the launch traced here: 112 us
  blocking collectives  75.6 us (67%)
  starting transfers between devices  19 us (17%)
  waiting for transfers between devices  12 us (11%)
  Pallas kernels  4.9 us (4%)
    all_gather x1, blocking collectives, local(): own = lax.all_gather(features, 'zo', axis=0, tiled=True)  53 us
    all_to_all x1, blocking collectives, local(): parts = lax.all_to_all(both, XY, 0, 0, tiled=True)  22.6 us
    ppermute x5, starting transfers between devices, turn(): lax.ppermute(array, Z + ('core',), [(2 * z + c, 2 * ((z + sign * (1 - 2 *...  12.4 us
    ppermute x5, waiting for transfers between devices, turn(): lax.ppermute(array, Z + ('core',), [(2 * z + c, 2 * ((z + sign * (1 - 2 *...  9.74 us
    ppermute x1, starting transfers between devices, local(): sibling = lax.ppermute(theirs, 'core', [(0, 1), (1, 0)])  6.59 us
    pallas_call x1, Pallas kernels, local(): pl.pallas_call(near_kernel, out_shape=(sums, *(jax.ShapeDtypeStruct(a.sha...  2.3 us
    ppermute x1, waiting for transfers between devices, local(): sibling = lax.ppermute(theirs, 'core', [(0, 1), (1, 0)])  2.26 us
  transfers between devices with their start and end apart: 6, of which 4 were waited for; matrix products, arithmetic and copies ran while one was open for 0% of the time, Pallas kernels for 2%

profile of v10, /device:TPU:1, one launch (start us, length us, event | category | flops | bytes accessed | tf_op | source)
XLA Modules:
  0.0 112.3 jit_solution(14958099163700984430)
XLA Ops:
  0.0 53.0 %all_gather.3.own_ref = bf16[512,512]{1,0:T(8,128)(2,1)S(1)} all-gather(bf16[64,512]{1,0:T(8,128)(2,1)} %param.6), channel_id=1, replica_groups=mesh['zo'=8,'zi'=4,'x'=4,'y'=4,'core'=2] {'zo'}, dimensions={0}, use_global_device_ids=true | all-gather | bytes 589824 | tf_op jit(solution)/shard_map/all_gather | solution.py:131
  53.0 1.9 %collective-permute-start = (bf16[320,512]{1,0:T(8,128)(2,1)S(1)}, bf16[320,512]{1,0:T(8,128)(2,1)S(1)}, u32[]{:S(2)}, u32[]{:S(2)}) collective-permute-start(bf16[320,512]{1,0:T(8,128)(2,1)S(1)} %slice.8), channel_id=1, source_target_pairs={{0,992},{1,33},{32,0},{33,65},{64,32},{65,97},{96,64},{97,129},{12... | collective-permute-start | bytes 983048 | tf_op jit(solution)/shard_map/ppermute | solution.py:121
  54.9 4.6 %collective-permute-start.2 = (bf16[512,512]{1,0:T(8,128)(2,1)S(1)}, bf16[512,512]{1,0:T(8,128)(2,1)S(1)}, u32[]{:S(2)}, u32[]{:S(2)}) collective-permute-start(bf16[512,512]{1,0:T(8,128)(2,1)S(1)} %all_gather.3.own_ref), channel_id=1, source_target_pairs={{0,32},{1,993},{32,64},{33,1},{64,96},{65,33},{96,128},{97,65},{12... | collective-permute-start | bytes 1572872 | tf_op jit(solution)/shard_map/ppermute | solution.py:121
  59.5 1.9 %collective-permute-start.1 = (bf16[192,512]{1,0:T(8,128)(2,1)S(1)}, bf16[192,512]{1,0:T(8,128)(2,1)S(1)}, u32[]{:S(2)}, u32[]{:S(2)}) collective-permute-start(bf16[192,512]{1,0:T(8,128)(2,1)S(1)} %slice.9), channel_id=1, source_target_pairs={{0,992},{1,33},{32,0},{33,65},{64,32},{65,97},{96,64},{97,129},{12... | collective-permute-start | bytes 589832 | tf_op jit(solution)/shard_map/ppermute | solution.py:121
  61.5 0.9 collective-permute-done.first_low_ref
  62.4 2.1 %collective-permute-start.3 = (bf16[320,512]{1,0:T(8,128)(2,1)S(1)}, bf16[320,512]{1,0:T(8,128)(2,1)S(1)}, u32[]{:S(2)}, u32[]{:S(2)}) collective-permute-start(bf16[320,512]{1,0:T(8,128)(2,1)S(1)} %collective-permute-done.first_low_ref), channel_id=1, source_target_pairs={{0,992},{1,33},{32,0},{33,65},{64,32},{65,97},{96,64},{97,129},{12... | collective-permute-start | bytes 983048 | tf_op jit(solution)/shard_map/ppermute | solution.py:121
  64.5 2.7 %collective-permute-done.1.first_high_ref = bf16[192,512]{1,0:T(8,128)(2,1)S(1)} collective-permute-done((bf16[192,512]{1,0:T(8,128)(2,1)S(1)}, bf16[192,512]{1,0:T(8,128)(2,1)S(1)}, u32[]{:S(2)}, u32[]{:S(2)}) %collective-permute-start.1) | collective-permute-done | bytes 196640 | tf_op jit(solution)/shard_map/ppermute | solution.py:121
  67.1 1.9 %collective-permute-start.4 = (bf16[192,512]{1,0:T(8,128)(2,1)S(1)}, bf16[192,512]{1,0:T(8,128)(2,1)S(1)}, u32[]{:S(2)}, u32[]{:S(2)}) collective-permute-start(bf16[192,512]{1,0:T(8,128)(2,1)S(1)} %collective-permute-done.1.first_high_ref), channel_id=1, source_target_pairs={{0,992},{1,33},{32,0},{33,65},{64,32},{65,97},{96,64},{97,129},{12... | collective-permute-start | bytes 589832 | tf_op jit(solution)/shard_map/ppermute | solution.py:121
  69.7 0.0 collective-permute-done.2.second_ref
  69.7 2.3 %shard_map.64 = (f32[2048,512]{1,0:T(8,128)S(1)}, bf16[1,1,16,128,128]{4,3,2,1,0:T(8,128)(2,1)S(1)}, s32[1,1,16]{2,1,0:T(1,128)S(1)}) custom-call(s32[1,1]{1,0:T(1,128)S(6)} %copy.9.count_ref, bf16[1,1,16,128,128]{4,3,2,1,0:T(8,128)(2,1)} %values_ref.1, s32[1,1,16]{2,1,0:T(1,128)} %index_ref.1, bf16[512,512]{1,0:T(8,128)(2,1)S(1)} %all_gather.3.own_ref, ...), custom_call_target="tpu_custom_call" | custom-call | flops 201326592 | bytes 6291456 | tf_op jit(solution)/shard_map/pallas_call | solution.py:153
  72.0 6.1 %collective-permute-done.4.far_high_ref = bf16[192,512]{1,0:T(8,128)(2,1)S(1)} collective-permute-done((bf16[192,512]{1,0:T(8,128)(2,1)S(1)}, bf16[192,512]{1,0:T(8,128)(2,1)S(1)}, u32[]{:S(2)}, u32[]{:S(2)}) %collective-permute-start.4) | collective-permute-done | bytes 196640 | tf_op jit(solution)/shard_map/ppermute | solution.py:121
  78.1 0.0 collective-permute-done.3.far_low_ref
  78.1 1.5 %shard_map.65 = (f32[2048,512]{1,0:T(8,128)S(1)}, bf16[16,64,512]{2,1,0:T(8,128)(2,1)S(1)}, f32[16,64,512]{2,1,0:T(8,128)S(1)}) custom-call(bf16[1,1,16,128,128]{4,3,2,1,0:T(8,128)(2,1)S(1)} %get-tuple-element.10.values_ref, s32[1,1,16]{2,1,0:T(1,128)S(1)} %get-tuple-element.11.index_ref, ...), custom_call_target="tpu_custom_call", output_to_operand_aliasing={{0}: (5, {})} | custom-call | flops 67108864 | bytes 2097152 | tf_op jit(solution)/shard_map/pallas_call | solution.py:175
  79.7 0.0 copy-start
  79.7 0.0 copy-start.1
  79.7 6.6 %collective-permute-start.5 = (bf16[16,64,512]{2,1,0:T(8,128)(2,1)S(1)}, bf16[16,64,512]{2,1,0:T(8,128)(2,1)S(1)}, u32[]{:S(2)}, u32[]{:S(2)}) collective-permute-start(bf16[16,64,512]{2,1,0:T(8,128)(2,1)S(1)} %get-tuple-element.14), channel_id=1, source_target_pairs={{0,1},{1,0},{2,3},{3,2},{4,5},{5,4},{6,7},{7,6},{8,9},{9,8},{10,11... | collective-permute-start | bytes 3145736 | tf_op jit(solution)/shard_map/ppermute | solution.py:185
  86.3 2.3 %collective-permute-done.5.sibling_ref = bf16[16,64,512]{2,1,0:T(8,128)(2,1)S(1)} collective-permute-done((bf16[16,64,512]{2,1,0:T(8,128)(2,1)S(1)}, bf16[16,64,512]{2,1,0:T(8,128)(2,1)S(1)}, u32[]{:S(2)}, u32[]{:S(2)}) %collective-permute-start.5) | collective-permute-done | bytes 1048608 | tf_op jit(solution)/shard_map/ppermute | solution.py:185
  88.5 0.2 shard_map.66
  88.7 22.6 %all_to_all.5.parts_ref = bf16[16,64,512]{2,1,0:T(8,128)(2,1)S(1)} all-to-all(bf16[16,64,512]{2,1,0:T(8,128)(2,1)S(1)} %shard_map.66), channel_id=1, replica_groups=mesh['zo'=8,'zi'=4,'x'=4,'y'=4,'core'=2] {'x','y'}, dimensions={0} | all-to-all | bytes 2097152 | tf_op jit(solution)/shard_map/all_to_all | solution.py:193
  111.3 0.0 copy-done
  111.3 0.0 copy-done.1
  111.3 0.9 shard_map.67
  (2 shorter events, 0.0 us)
Async XLA Ops:
  53.0 9.4 %collective-permute-start = (bf16[320,512]{1,0:T(8,128)(2,1)S(1)}, bf16[320,512]{1,0:T(8,128)(2,1)S(1)}, u32[]{:S(2)}, u32[]{:S(2)}) collective-permute-start(bf16[320,512]{1,0:T(8,128)(2,1)S(1)} %slice.8), channel_id=1, source_target_pairs={{0,992},{1,33},{32,0},{33,65},{64,32},{65,97},{96,64},{97,129},{12... | collective-permute-start | bytes 983048 | tf_op jit(solution)/shard_map/ppermute | solution.py:121
  54.9 14.8 %collective-permute-start.2 = (bf16[512,512]{1,0:T(8,128)(2,1)S(1)}, bf16[512,512]{1,0:T(8,128)(2,1)S(1)}, u32[]{:S(2)}, u32[]{:S(2)}) collective-permute-start(bf16[512,512]{1,0:T(8,128)(2,1)S(1)} %all_gather.3.own_ref), channel_id=1, source_target_pairs={{0,32},{1,993},{32,64},{33,1},{64,96},{65,33},{96,128},{97,65},{12... | collective-permute-start | bytes 1572872 | tf_op jit(solution)/shard_map/ppermute | solution.py:121
  59.5 7.6 %collective-permute-start.1 = (bf16[192,512]{1,0:T(8,128)(2,1)S(1)}, bf16[192,512]{1,0:T(8,128)(2,1)S(1)}, u32[]{:S(2)}, u32[]{:S(2)}) collective-permute-start(bf16[192,512]{1,0:T(8,128)(2,1)S(1)} %slice.9), channel_id=1, source_target_pairs={{0,992},{1,33},{32,0},{33,65},{64,32},{65,97},{96,64},{97,129},{12... | collective-permute-start | bytes 589832 | tf_op jit(solution)/shard_map/ppermute | solution.py:121
  62.4 15.7 %collective-permute-start.3 = (bf16[320,512]{1,0:T(8,128)(2,1)S(1)}, bf16[320,512]{1,0:T(8,128)(2,1)S(1)}, u32[]{:S(2)}, u32[]{:S(2)}) collective-permute-start(bf16[320,512]{1,0:T(8,128)(2,1)S(1)} %collective-permute-done.first_low_ref), channel_id=1, source_target_pairs={{0,992},{1,33},{32,0},{33,65},{64,32},{65,97},{96,64},{97,129},{12... | collective-permute-start | bytes 983048 | tf_op jit(solution)/shard_map/ppermute | solution.py:121
  67.1 11.0 %collective-permute-start.4 = (bf16[192,512]{1,0:T(8,128)(2,1)S(1)}, bf16[192,512]{1,0:T(8,128)(2,1)S(1)}, u32[]{:S(2)}, u32[]{:S(2)}) collective-permute-start(bf16[192,512]{1,0:T(8,128)(2,1)S(1)} %collective-permute-done.1.first_high_ref), channel_id=1, source_target_pairs={{0,992},{1,33},{32,0},{33,65},{64,32},{65,97},{96,64},{97,129},{12... | collective-permute-start | bytes 589832 | tf_op jit(solution)/shard_map/ppermute | solution.py:121
  79.7 31.7 %copy-start = (bf16[512,512]{1,0:T(8,128)(2,1)S(1)}, bf16[512,512]{1,0:T(8,128)(2,1)}, u32[]{:S(2)}) copy-start(bf16[512,512]{1,0:T(8,128)(2,1)} %weight_ref.1) | copy-start | bytes 1572868
  79.7 31.7 %copy-start.1 = (f32[512]{0:T(512)S(1)}, f32[512]{0:T(512)}, u32[]{:S(2)}) copy-start(f32[512]{0:T(512)} %param.11) | copy-start | bytes 6148
  79.7 8.9 %collective-permute-start.5 = (bf16[16,64,512]{2,1,0:T(8,128)(2,1)S(1)}, bf16[16,64,512]{2,1,0:T(8,128)(2,1)S(1)}, u32[]{:S(2)}, u32[]{:S(2)}) collective-permute-start(bf16[16,64,512]{2,1,0:T(8,128)(2,1)S(1)} %get-tuple-element.14), channel_id=1, source_target_pairs={{0,1},{1,0},{2,3},{3,2},{4,5},{5,4},{6,7},{7,6},{8,9},{9,8},{10,11... | collective-permute-start | bytes 3145736 | tf_op jit(solution)/shard_map/ppermute | solution.py:185
